TPU v7x, 512 devices: a whole 4x4x16 slice. The times are simulated.
512 devices in a mesh: dp: 4 (over x_lo, core), expert: 16 (over z), tensor: 8 (over x_hi, y).
Axes of the slice: x: 4 (x_hi: 2, x_lo: 2; x = x_hi * 2 + x_lo), y: 4, z: 16, core: 2. Of those that a mesh axis runs over, the one named last changes fastest.
Arguments:
- tokens: bfloat16 [8192, 2048], P(('dp', 'expert')), may hold values from -6 to 6
- routes: int32 [8192], P(('dp', 'expert')), may hold values from 0 to 15, as said below
- slots: int32 [8192], P(('dp', 'expert')), may hold values from 0 to 16, as said below
- gate: float32 [8192], P(('dp', 'expert')), may hold values from 0.25 to 1
- cotangent: bfloat16 [8192, 2048], P(('dp', 'expert')), may hold values from -6 to 6
- w_in: bfloat16 [16, 2048, 8192], P('expert', 'dp', 'tensor'), may hold values from -0.125 to 0.125
- w_out: bfloat16 [16, 8192, 2048], P('expert', 'tensor', 'dp'), may hold values from -0.0625 to 0.0625
Outputs:
- grad_tokens: bfloat16 [8192, 2048], P(('dp', 'expert'))
- grad_w_in: bfloat16 [16, 2048, 8192], P('expert', 'dp', 'tensor')
- grad_w_out: bfloat16 [16, 8192, 2048], P('expert', 'tensor', 'dp')
Inputs may be any that keep to these rules, and one draw needn't show every extreme that they name: `routes`: in the 128 tokens of every group (rows held by one index of dp+expert) every expert is named; in every data replica one expert is named by more than 16 tokens of each of its groups. The kept tokens of one group and one expert take slots 0, 1, 2, ... in token order; the value 16 marks a dropped token, and every group drops some token.
All inputs are finite; a program needn't handle non-finite values.
Results may differ from a plain program's by a relative error of at most 0.0058.
Values may be sent and summed in bfloat16 or wider, within the bound.
No kernel may reach another device: no remote copies, remote signals or barrier semaphores. Data moves between devices by JAX's collectives and lax.ppermute only.
A program may use at most 64 MiB of HBM per device.

v0:
```python
import jax
import jax.numpy as jnp
from jax import lax
from jax.sharding import PartitionSpec as P


def gelu_parts(preact):
    normal_cdf = 0.5 * (1.0 + jax.scipy.special.erf(preact * 0.7071067811865476))
    density = jnp.exp(-0.5 * preact * preact) * 0.3989422804014327
    return (preact * normal_cdf, normal_cdf + preact * density)


def route_table(routes, slots, first, count, experts_count, capacity):
    local = slots - first
    inside = (slots < capacity) & (local >= 0) & (local < count)
    position = jnp.where(inside, routes * count + local, -1)
    targets = lax.broadcasted_iota(jnp.int32, (experts_count * count, routes.shape[0]), 0)
    return (targets == position[None, :]).astype(jnp.bfloat16)


def contract_rows(left, right):
    return lax.dot_general(
        left, right, (((0,), (0,)), ((), ())), preferred_element_type=jnp.float32
    )


def contract_cols(left, right):
    return lax.dot_general(
        left, right, (((1,), (1,)), ((), ())), preferred_element_type=jnp.float32
    )


def combine_rows(row_grads):
    return lax.all_to_all(row_grads, "expert", split_axis=0, concat_axis=0, tiled=True)


def tensor_total(partial_value):
    return lax.psum(partial_value, "tensor")


def shards(tokens, routes, slots, gate, cotangent, w_in, w_out):
    experts_count = lax.axis_size("expert")
    group_size = tokens.shape[0]
    model_width = tokens.shape[1]
    capacity = 2 * group_size // experts_count
    row_count = experts_count * capacity
    scaled = (cotangent.astype(jnp.float32) * gate[:, None]).astype(jnp.bfloat16)
    full_table = route_table(routes, slots, 0, capacity, experts_count, capacity)
    sent_tokens = jnp.dot(full_table, tokens, preferred_element_type=jnp.float32).astype(
        jnp.bfloat16
    )
    sent_grads = jnp.dot(full_table, scaled, preferred_element_type=jnp.float32).astype(
        jnp.bfloat16
    )
    sent_tokens = sent_tokens.reshape(experts_count, capacity, model_width)
    sent_grads = sent_grads.reshape(experts_count, capacity, model_width)
    tok_buffer, grad_buffer = (
        lax.all_to_all(sent_tokens, "expert", split_axis=0, concat_axis=0, tiled=True),
        lax.all_to_all(sent_grads, "expert", split_axis=0, concat_axis=0, tiled=True),
    )
    tok_rows = tok_buffer.reshape(row_count, model_width)
    grad_rows = grad_buffer.reshape(row_count, model_width)
    first_full, second_full = (
        lax.all_gather(w_in[0], "dp", axis=0, tiled=True),
        lax.all_gather(w_out[0], "dp", axis=1, tiled=True),
    )
    preact = jnp.dot(tok_rows, first_full, preferred_element_type=jnp.float32)
    value, slope = gelu_parts(preact)
    hidden = value.astype(jnp.bfloat16)
    grad_hidden = contract_cols(grad_rows, second_full)
    grad_pre = (grad_hidden * slope).astype(jnp.bfloat16)
    token_slices, grad_slices = (
        lax.all_to_all(tok_rows, "dp", split_axis=1, concat_axis=0, tiled=True),
        lax.all_to_all(grad_rows, "dp", split_axis=1, concat_axis=0, tiled=True),
    )
    grad_first = contract_rows(token_slices, lax.all_gather(grad_pre, "dp", axis=0, tiled=True))
    grad_second = contract_rows(lax.all_gather(hidden, "dp", axis=0, tiled=True), grad_slices)
    partial_value = contract_cols(grad_pre, first_full).reshape(
        experts_count, capacity, model_width
    )
    row_grads = tensor_total(partial_value).astype(jnp.bfloat16)
    returned_rows = combine_rows(row_grads).reshape(row_count, model_width)
    grad_tokens = contract_rows(full_table, returned_rows).astype(jnp.bfloat16)
    return (
        grad_tokens,
        grad_first.astype(jnp.bfloat16)[None],
        grad_second.astype(jnp.bfloat16)[None],
    )


def solution(mesh):
    return jax.shard_map(
        shards,
        mesh=mesh,
        in_specs=(
            P(("dp", "expert"), None),
            P(("dp", "expert")),
            P(("dp", "expert")),
            P(("dp", "expert")),
            P(("dp", "expert"), None),
            P("expert", "dp", "tensor"),
            P("expert", "tensor", "dp"),
        ),
        out_specs=(
            P(("dp", "expert"), None),
            P("expert", "dp", "tensor"),
            P("expert", "tensor", "dp"),
        ),
        check_vma=False,
    )
```

profile of v0, /device:TPU:1, one launch (start us, length us, event | category | flops | bytes accessed | tf_op | source)
XLA Modules:
  0.0 321.8 jit_solution(12192465263531151175)
XLA Ops:
  7.2 0.7 all-gather.13.cloned.1.call-update
  8.6 1.4 convolution_convert_fusion
  10.0 15.7 %all-to-all-start.1 = ((bf16[16,16,2048]{2,1,0:T(8,128)(2,1)}), bf16[16,16,2048]{2,1,0:T(8,128)(2,1)S(1)}, u32[]{:S(2)}, u32[]{:S(2)}) async-start(bf16[16,16,2048]{2,1,0:T(8,128)(2,1)} %bitcast.3), calls=%async_computation.1 | async-start | bytes 2097152 | tf_op jit(solution)/shard_map/all_to_all | solution.py:58
  25.8 0.7 all-gather.11.cloned.1.call-update
  26.5 1.5 convolution_convert_fusion.1
  28.0 42.6 %all-to-all-done.1 = bf16[16,16,2048]{2,1,0:T(8,128)(2,1)S(1)} async-done(((bf16[16,16,2048]{2,1,0:T(8,128)(2,1)}), bf16[16,16,2048]{2,1,0:T(8,128)(2,1)S(1)}, u32[]{:S(2)}, u32[]{:S(2)}) %all-to-all-start.1) | async-done | bytes 1048608 | tf_op jit(solution)/shard_map/all_to_all | solution.py:58
  70.6 13.2 %all-to-all-start = ((bf16[16,16,2048]{2,1,0:T(8,128)(2,1)}), bf16[16,16,2048]{2,1,0:T(8,128)(2,1)S(1)}, u32[]{:S(2)}, u32[]{:S(2)}) async-start(bf16[16,16,2048]{2,1,0:T(8,128)(2,1)} %bitcast.42), calls=%async_computation | async-start | bytes 2097152 | tf_op jit(solution)/shard_map/all_to_all | solution.py:59
  83.8 1.6 all_to_all.40
  85.4 2.4 copy.12
  87.8 4.9 %multiply_convert_fusion = (bf16[256,1024]{1,0:T(8,128)(2,1)}, f32[256,1024]{1,0:T(8,128)}) fusion(bf16[256,2048]{1,0:T(8,128)(2,1)S(1)} %bitcast.41, bf16[1,2048,1024]{2,1,0:T(8,128)(2,1)} %all-gather.13.cloned.1.call-done), kind=kOutput, calls=%fused_computation.20 | convolution fusion | flops 1075052544 | bytes 6815744 | tf_op jit(solution)/shard_map/dot_general | solution.py:67
  92.7 36.4 %all-to-all-done = bf16[16,16,2048]{2,1,0:T(8,128)(2,1)S(1)} async-done(((bf16[16,16,2048]{2,1,0:T(8,128)(2,1)}), bf16[16,16,2048]{2,1,0:T(8,128)(2,1)S(1)}, u32[]{:S(2)}, u32[]{:S(2)}) %all-to-all-start) | async-done | bytes 1048608 | tf_op jit(solution)/shard_map/all_to_all | solution.py:59
  129.0 9.8 %all-to-all-start.3 = ((bf16[256,4,512]{2,0,1:T(8,128)(2,1)}), bf16[256,4,512]{2,0,1:T(8,128)(2,1)}, u32[]{:S(2)}, u32[]{:S(2)}) async-start(bf16[256,4,512]{2,0,1:T(8,128)(2,1)} %copy.12), calls=%async_computation.3 | async-start | bytes 2097152 | tf_op jit(solution)/shard_map/all_to_all | solution.py:73
  138.9 4.5 %fusion.11 = bf16[256,1024]{1,0:T(8,128)(2,1)} fusion(bf16[256,2048]{1,0:T(8,128)(2,1)S(1)} %bitcast.39, bf16[1,1024,2048]{2,1,0:T(8,128)(2,1)} %all-gather.11.cloned.1.call-done, f32[256,1024]{1,0:T(8,128)S(1)} %copy-done.4), kind=kOutput, calls=%fused_computation.15 | convolution fusion | flops 1076363264 | bytes 6815744 | tf_op jit(solution)/shard_map/dot_general | solution.py:28
  143.4 0.8 all_to_all.44
  144.2 1.2 copy.13
  145.4 3.5 %fusion = f32[256,2048]{1,0:T(8,128)S(1)} fusion(bf16[256,1024]{1,0:T(8,128)(2,1)S(1)} %copy-done.1, bf16[1,2048,1024]{2,1,0:T(8,128)(2,1)} %all-gather.13.cloned.1.call-done), kind=kOutput, calls=%fused_computation | convolution fusion | flops 1073741824 | bytes 6815744 | tf_op jit(solution)/shard_map/dot_general | solution.py:28
  148.9 3.7 %all-to-all-done.3 = bf16[256,4,512]{2,0,1:T(8,128)(2,1)} async-done(((bf16[256,4,512]{2,0,1:T(8,128)(2,1)}), bf16[256,4,512]{2,0,1:T(8,128)(2,1)}, u32[]{:S(2)}, u32[]{:S(2)}) %all-to-all-start.3) | async-done | bytes 1048608 | tf_op jit(solution)/shard_map/all_to_all | solution.py:73
  152.6 5.1 %all-to-all-start.4 = ((bf16[256,4,512]{2,0,1:T(8,128)(2,1)}), bf16[256,4,512]{2,0,1:T(8,128)(2,1)}, u32[]{:S(2)}, u32[]{:S(2)}) async-start(bf16[256,4,512]{2,0,1:T(8,128)(2,1)} %copy.13), calls=%async_computation.4 | async-start | bytes 2097152 | tf_op jit(solution)/shard_map/all_to_all | solution.py:74
  157.7 95.5 %all-reduce.1 = bf16[16,16,2048]{2,1,0:T(8,128)(2,1)} all-reduce(f32[16,16,2048]{2,1,0:T(8,128)S(1)} %bitcast.43), channel_id=1, replica_groups=mesh['dp'=4,'expert'=16,'tensor'=8] {'tensor'}, use_global_device_ids=true, to_apply=%region_0.1 | all-reduce | flops 524288 | bytes 3145728 | tf_op jit(solution)/shard_map/psum | solution.py:38
  253.2 6.4 %all-to-all-start.2 = ((bf16[16,16,2048]{2,1,0:T(8,128)(2,1)}), bf16[16,16,2048]{2,1,0:T(8,128)(2,1)S(1)}, u32[]{:S(2)}, u32[]{:S(2)}) async-start(bf16[16,16,2048]{2,1,0:T(8,128)(2,1)} %all-reduce.1), calls=%async_computation.2 | async-start | bytes 2097152 | tf_op jit(solution)/shard_map/all_to_all | solution.py:34
  260.2 4.2 %fusion.6 = bf16[1,512,1024]{2,1,0:T(8,128)(2,1)} fusion(bf16[1024,512]{1,0:T(8,128)(2,1)} %bitcast.9, bf16[1024,1024]{1,0:T(8,128)(2,1)} %all-gather.7.cloned.1.call-done), kind=kOutput, calls=%fused_computation.12 | convolution fusion | flops 1074266112 | bytes 4194304 | tf_op jit(solution)/shard_map/dot_general | solution.py:22
  264.4 45.6 %all-gather.9.cloned.1.call-done = bf16[1024,1024]{1,0:T(8,128)(2,1)} async-done(((bf16[256,1024]{1,0:T(8,128)(2,1)}), bf16[1024,1024]{1,0:T(8,128)(2,1)}) %all-gather.9.cloned.1.call-update) | async-done | bytes 2097168 | tf_op jit(solution)/shard_map/all_gather | solution.py:77
  310.0 4.1 %fusion.7 = bf16[1,1024,512]{2,1,0:T(8,128)(2,1)} fusion(bf16[1024,1024]{1,0:T(8,128)(2,1)} %all-gather.9.cloned.1.call-done, bf16[1024,512]{1,0:T(8,128)(2,1)} %bitcast.12), kind=kOutput, calls=%fused_computation.13 | convolution fusion | flops 1074266112 | bytes 4194304 | tf_op jit(solution)/shard_map/dot_general | solution.py:22
  314.1 1.1 convolution_convert_fusion.2
  (22 shorter events, 1.4 us)
Async XLA Ops:
  7.2 1.4 copy-start
  7.2 80.6 %all-gather.13.cloned.1.call-start = ((), (), s32[]{:S(2)}) async-start(), calls=%async_computation.8 | async-start | bytes 5242880 | tf_op jit(solution)/shard_map/all_gather | solution.py:64
  8.6 17.9 %copy-start.2 = (bf16[128,2048]{1,0:T(8,128)(2,1)S(1)}, bf16[128,2048]{1,0:T(8,128)(2,1)}, u32[]{:S(2)}) copy-start(bf16[128,2048]{1,0:T(8,128)(2,1)} %param.11) | copy-start | bytes 1572868
  8.6 17.9 %copy-start.3 = (f32[128]{0:T(128)S(1)}, f32[128]{0:T(128)}, u32[]{:S(2)}) copy-start(f32[128]{0:T(128)} %param.10) | copy-start | bytes 1540
  10.0 60.6 %all-to-all-start.1 = ((bf16[16,16,2048]{2,1,0:T(8,128)(2,1)}), bf16[16,16,2048]{2,1,0:T(8,128)(2,1)S(1)}, u32[]{:S(2)}, u32[]{:S(2)}) async-start(bf16[16,16,2048]{2,1,0:T(8,128)(2,1)} %bitcast.3), calls=%async_computation.1 | async-start | bytes 2097152 | tf_op jit(solution)/shard_map/all_to_all | solution.py:58
  25.8 113.1 %all-gather.11.cloned.1.call-start = ((), (), s32[]{:S(2)}) async-start(), calls=%async_computation.7 | async-start | bytes 5242880 | tf_op jit(solution)/shard_map/all_gather | solution.py:65
  70.6 58.4 %all-to-all-start = ((bf16[16,16,2048]{2,1,0:T(8,128)(2,1)}), bf16[16,16,2048]{2,1,0:T(8,128)(2,1)S(1)}, u32[]{:S(2)}, u32[]{:S(2)}) async-start(bf16[16,16,2048]{2,1,0:T(8,128)(2,1)} %bitcast.42), calls=%async_computation | async-start | bytes 2097152 | tf_op jit(solution)/shard_map/all_to_all | solution.py:59
  92.7 46.2 %copy-start.4 = (f32[256,1024]{1,0:T(8,128)S(1)}, f32[256,1024]{1,0:T(8,128)}, u32[]{:S(2)}) copy-start(f32[256,1024]{1,0:T(8,128)} %get-tuple-element.4) | copy-start | bytes 3145732
  129.0 23.6 %all-to-all-start.3 = ((bf16[256,4,512]{2,0,1:T(8,128)(2,1)}), bf16[256,4,512]{2,0,1:T(8,128)(2,1)}, u32[]{:S(2)}, u32[]{:S(2)}) async-start(bf16[256,4,512]{2,0,1:T(8,128)(2,1)} %copy.12), calls=%async_computation.3 | async-start | bytes 2097152 | tf_op jit(solution)/shard_map/all_to_all | solution.py:73
  138.9 121.3 %all-gather.7.cloned.1.call-start = ((), (), s32[]{:S(2)}) async-start(), calls=%async_computation.5 | async-start | bytes 2621440 | tf_op jit(solution)/shard_map/all_gather | solution.py:76
  143.4 2.0 copy-start.1
  152.6 100.6 %all-to-all-start.4 = ((bf16[256,4,512]{2,0,1:T(8,128)(2,1)}), bf16[256,4,512]{2,0,1:T(8,128)(2,1)}, u32[]{:S(2)}, u32[]{:S(2)}) async-start(bf16[256,4,512]{2,0,1:T(8,128)(2,1)} %copy.13), calls=%async_computation.4 | async-start | bytes 2097152 | tf_op jit(solution)/shard_map/all_to_all | solution.py:74
  253.2 60.9 %all-to-all-start.2 = ((bf16[16,16,2048]{2,1,0:T(8,128)(2,1)}), bf16[16,16,2048]{2,1,0:T(8,128)(2,1)S(1)}, u32[]{:S(2)}, u32[]{:S(2)}) async-start(bf16[16,16,2048]{2,1,0:T(8,128)(2,1)} %all-reduce.1), calls=%async_computation.2 | async-start | bytes 2097152 | tf_op jit(solution)/shard_map/all_to_all | solution.py:34
  259.6 50.4 %all-gather.9.cloned.1.call-start = ((), (), s32[]{:S(2)}) async-start(), calls=%async_computation.6 | async-start | bytes 2621440 | tf_op jit(solution)/shard_map/all_gather | solution.py:77
Sparse Core Ops, SparseCore 0:
  10.1 60.1 all-gather.12
  72.4 55.3 all-gather.10
  143.5 48.2 all-gather.6
  262.8 47.1 all-gather.8
where the time goes:
time: 322 us
  waiting for transfers between devices  130 us (40%)
  blocking collectives  95.5 us (30%)
  starting transfers between devices  50.4 us (16%)
  matrix products  25.1 us (8%)
  between operations  13.9 us (4%)
  local copies, waits for them, and re-layouts  5.98 us (2%)
    psum x1, blocking collectives, tensor_total(): return lax.psum(partial_value, 'tensor')  95.5 us
    all_gather x1, waiting for transfers between devices, shards(): lax.all_gather(hidden, 'dp', axis=0, tiled=True)  45.6 us
    all_to_all x1, waiting for transfers between devices, shards(): lax.all_to_all(sent_tokens, 'expert', split_axis=0, concat_axis=0, tiled=...  42.6 us
    all_to_all x1, waiting for transfers between devices, shards(): lax.all_to_all(sent_grads, 'expert', split_axis=0, concat_axis=0, tiled=T...  36.4 us
    all_to_all x1, starting transfers between devices, shards(): lax.all_to_all(sent_tokens, 'expert', split_axis=0, concat_axis=0, tiled=...  15.7 us
    all_to_all x1, starting transfers between devices, shards(): lax.all_to_all(sent_grads, 'expert', split_axis=0, concat_axis=0, tiled=T...  13.2 us
    all_to_all x1, starting transfers between devices, shards(): lax.all_to_all(tok_rows, 'dp', split_axis=1, concat_axis=0, tiled=True)  9.85 us
    dot_general x3, matrix products, contract_rows(): lax.dot_general(left, right, (((0,), (0,)), ((), ())), preferred_element_...  9.42 us
  transfers between devices with their start and end apart: 9, of which 4 were waited for; matrix products, arithmetic and copies ran while one was open for 9% of the time, Pallas kernels for 0%

commit v1 on v0

v1 whole, which is shorter than its diff:
```python
import jax
import jax.numpy as jnp
from jax import lax
from jax.experimental import pallas as pl
from jax.experimental.pallas import tpu as pltpu
from jax.sharding import PartitionSpec as P

ACROSS = [(0, 2), (2, 0), (1, 3), (3, 1)]
BESIDE = [(0, 1), (1, 0), (2, 3), (3, 2)]
DIAGONAL = [(0, 3), (3, 0), (1, 2), (2, 1)]
VMEM_BYTES = 48 * 1024 * 1024


def gelu_parts(preact):
    normal_cdf = 0.5 * (1.0 + lax.erf(preact * 0.7071067811865476))
    density = jnp.exp(-0.5 * preact * preact) * 0.3989422804014327
    return (preact * normal_cdf, normal_cdf + preact * density)


def route_table(routes, slots, experts_count, capacity):
    position = jnp.where(slots < capacity, routes * capacity + slots, -1)
    targets = lax.broadcasted_iota(jnp.int32, (experts_count * capacity, routes.shape[0]), 0)
    return (targets == position[None, :]).astype(jnp.bfloat16)


def dot(left, right, left_dim, right_dim):
    return lax.dot_general(
        left,
        right,
        (((left_dim,), (right_dim,)), ((), ())),
        preferred_element_type=jnp.float32,
    )


def hidden_kernel(rows_ref, *refs):
    first, second = refs[0:4], refs[4:8]
    acts_ref, sent_ref, total = refs[8:11]
    step, steps = pl.program_id(0), pl.num_programs(0)
    block = rows_ref.shape[3]
    halves = first[0].shape[0] // block
    blocks = range(rows_ref.shape[0])

    def weight_in(t):
        return first[t // halves][pl.ds((t % halves) * block, block), :]

    def weight_out(t):
        return second[t // halves][:, pl.ds((t % halves) * block, block)]

    preact = sum(dot(rows_ref[t, 0], weight_in(t), 1, 0) for t in blocks)
    grad_hidden = sum(dot(rows_ref[t, 1], weight_out(t), 1, 1) for t in blocks)
    value, slope = gelu_parts(preact)
    grad_pre = (grad_hidden * slope).astype(jnp.bfloat16)
    acts_ref[0] = value.astype(jnp.bfloat16)
    acts_ref[1] = grad_pre

    @pl.when(step == 0)
    def _():
        for t in blocks:
            total[t] = dot(grad_pre, weight_in(t), 1, 1)

    @pl.when(step > 0)
    def _():
        for t in blocks:
            total[t] += dot(grad_pre, weight_in(t), 1, 1)

    @pl.when(step == steps - 1)
    def _():
        sent_ref[...] = total[...].astype(jnp.bfloat16)


def hidden_layer(rows, first, second):
    blocks, _, count, block = rows.shape
    depth, width = first[0].shape
    tile = 256
    flops = 3 * 2 * count * blocks * block * width
    return pl.pallas_call(
        hidden_kernel,
        grid=(width // tile,),
        in_specs=[pl.BlockSpec(rows.shape, lambda j: (0, 0, 0, 0))]
        + [pl.BlockSpec((depth, tile), lambda j: (0, j))] * 4
        + [pl.BlockSpec((tile, depth), lambda j: (j, 0))] * 4,
        out_specs=[
            pl.BlockSpec((2, count, tile), lambda j: (0, 0, j)),
            pl.BlockSpec((blocks, count, block), lambda j: (0, 0, 0)),
        ],
        out_shape=[
            jax.ShapeDtypeStruct((2, count, width), jnp.bfloat16),
            jax.ShapeDtypeStruct((blocks, count, block), jnp.bfloat16),
        ],
        scratch_shapes=[pltpu.VMEM((blocks, count, block), jnp.float32)],
        compiler_params=pltpu.CompilerParams(vmem_limit_bytes=VMEM_BYTES),
        cost_estimate=pl.CostEstimate(
            flops=flops, bytes_accessed=13 * 1024 * 1024, transcendentals=2 * count * width
        ),
        name="hidden_layer",
    )(rows, *first, *second)


def weights_kernel(*refs):
    rows, acts = refs[0:4], refs[4:8]
    first_ref, second_ref = refs[8:10]
    block = rows[0].shape[3]
    for b in range(rows[0].shape[0]):
        first_ref[pl.ds(b * block, block), :] = sum(
            dot(rows[k][b, 0], acts[k][1], 0, 0) for k in range(4)
        ).astype(jnp.bfloat16)
        second_ref[:, pl.ds(b * block, block)] = sum(
            dot(acts[k][0], rows[k][b, 1], 0, 0) for k in range(4)
        ).astype(jnp.bfloat16)


def weight_grads(rows, acts):
    _, _, count, block = rows[0].shape
    width = acts[0].shape[2]
    tile, depth = 256, 2 * block
    flops = 2 * 2 * 4 * count * depth * width
    return pl.pallas_call(
        weights_kernel,
        grid=(width // tile,),
        in_specs=[pl.BlockSpec((2, 2, count, block), lambda j: (0, 0, 0, 0))] * 4
        + [pl.BlockSpec((2, count, tile), lambda j: (0, 0, j))] * 4,
        out_specs=[
            pl.BlockSpec((depth, tile), lambda j: (0, j)),
            pl.BlockSpec((tile, depth), lambda j: (j, 0)),
        ],
        out_shape=[
            jax.ShapeDtypeStruct((depth, width), jnp.bfloat16),
            jax.ShapeDtypeStruct((width, depth), jnp.bfloat16),
        ],
        compiler_params=pltpu.CompilerParams(vmem_limit_bytes=VMEM_BYTES),
        cost_estimate=pl.CostEstimate(
            flops=flops, bytes_accessed=8 * 1024 * 1024, transcendentals=0
        ),
        name="weight_grads",
    )(*rows, *acts)


def shards(tokens, routes, slots, gate, cotangent, w_in, w_out):
    experts = lax.axis_size("expert")
    parts = lax.axis_size("tensor")
    group, model_width = tokens.shape
    capacity = 2 * group // experts
    count = experts * capacity
    block = model_width // parts
    replica = lax.axis_index("dp")
    part = lax.axis_index("tensor")
    halves = parts // 4

    start = ((replica ^ (part // halves)) * halves + part % halves) * block
    own_tokens = lax.dynamic_slice_in_dim(tokens, start, block, 1)
    own_cotangent = lax.dynamic_slice_in_dim(cotangent, start, block, 1)
    scaled = (own_cotangent.astype(jnp.float32) * gate[:, None]).astype(jnp.bfloat16)
    table = route_table(routes, slots, experts, capacity)
    sent_tokens = dot(table, own_tokens, 1, 0).astype(jnp.bfloat16)
    sent_grads = dot(table, scaled, 1, 0).astype(jnp.bfloat16)
    sent = jnp.concatenate(
        [
            sent_tokens.reshape(experts, capacity, block),
            sent_grads.reshape(experts, capacity, block),
        ],
        axis=1,
    )
    came = lax.all_to_all(sent, "expert", 0, 0, tiled=True)
    came = came.reshape(experts, 2, capacity, block).transpose(1, 0, 2, 3)
    came = came.reshape(2, count, block)
    rows = lax.all_to_all(
        jnp.broadcast_to(came[None], (parts, 2, count, block)), "tensor", 0, 0, tiled=True
    )

    first0, second0 = w_in[0], w_out[0]
    first2, second2 = lax.ppermute(first0, "dp", ACROSS), lax.ppermute(second0, "dp", ACROSS)
    first1, second1 = lax.ppermute(first0, "dp", BESIDE), lax.ppermute(second0, "dp", BESIDE)
    first3, second3 = lax.ppermute(first2, "dp", BESIDE), lax.ppermute(second2, "dp", BESIDE)

    acts0, partial_rows = hidden_layer(
        rows, (first0, first1, first2, first3), (second0, second1, second2, second3)
    )

    terms = lax.all_to_all(partial_rows, "tensor", 0, 0, tiled=True)
    row_grads = jnp.sum(terms.astype(jnp.float32), axis=0).astype(jnp.bfloat16)
    returned = lax.all_to_all(
        row_grads.reshape(experts, capacity, block), "expert", 0, 0, tiled=True
    ).reshape(count, block)
    own_grads = dot(table, returned, 0, 0).astype(jnp.bfloat16)
    pieces = lax.all_to_all(
        jnp.broadcast_to(own_grads[None], (parts, group, block)), "tensor", 0, 0, tiled=True
    )
    pieces = pieces.reshape(2, 2, halves, group, block)
    pieces = jnp.where(replica // 2 == 1, pieces[::-1], pieces)
    pieces = jnp.where(replica % 2 == 1, pieces[:, ::-1], pieces)
    grad_tokens = pieces.reshape(parts, group, block).transpose(1, 0, 2).reshape(group, model_width)

    rows1 = lax.ppermute(rows[halves : 2 * halves], "dp", BESIDE)
    rows2 = lax.ppermute(rows[2 * halves : 3 * halves], "dp", ACROSS)
    rows3 = lax.ppermute(rows[3 * halves :], "dp", DIAGONAL)
    acts2 = lax.ppermute(acts0, "dp", ACROSS)
    acts1 = lax.ppermute(acts0, "dp", BESIDE)
    acts3 = lax.ppermute(acts2, "dp", BESIDE)
    grad_first, grad_second = weight_grads((rows, rows1, rows2, rows3), (acts0, acts1, acts2, acts3))
    return grad_tokens, grad_first[None], grad_second[None]


def solution(mesh):
    return jax.shard_map(
        shards,
        mesh=mesh,
        in_specs=(
            P(("dp", "expert"), None),
            P(("dp", "expert")),
            P(("dp", "expert")),
            P(("dp", "expert")),
            P(("dp", "expert"), None),
            P("expert", "dp", "tensor"),
            P("expert", "tensor", "dp"),
        ),
        out_specs=(
            P(("dp", "expert"), None),
            P("expert", "dp", "tensor"),
            P("expert", "tensor", "dp"),
        ),
        check_vma=False,
    )
```

time: 322 us -> 198 us (0.61)
  blocking collectives: 95.5 us -> 0 us
  waiting for transfers between devices: 130 us -> 68.1 us
  starting transfers between devices: 50.4 us -> 94.2 us
  matrix products: 25.1 us -> 1.49 us
  Pallas kernels: 0 us -> 14.7 us
  between operations: 13.9 us -> 0.9 us
  local copies, waits for them, and re-layouts: 5.98 us -> 12.4 us
  other arithmetic: 0.68 us -> 4.98 us
    psum x1 -> x0, blocking collectives: 95.5 us -> none  [tensor_total(): return lax.psum(partial_value, 'tensor')]
    ppermute x0 -> x12, starting transfers between devices: none -> 49.1 us  [the longest x1 8.53 us: shards(): acts1 = lax.ppermute(acts0, 'dp', BESIDE)]
    all_to_all x5, waiting for transfers between devices: 82.7 us -> 35.6 us  [the longest x1 16.5 us: shards(): lax.all_to_all(jnp.broadcast_to(came[None], (parts, 2, count, block)), 't...]
    all_gather x4 -> x0, waiting for transfers between devices: 45.6 us -> none  [the longest x1 45.6 us: shards(): lax.all_gather(hidden, 'dp', axis=0, tiled=True)]
    ppermute x0 -> x12, waiting for transfers between devices: none -> 32.5 us  [the longest x1 13.2 us: shards(): lax.ppermute(second0, 'dp', ACROSS)]
    dot_general x8 -> x3, matrix products: 25.1 us -> 1.49 us  [dot(): lax.dot_general(left, right, (((left_dim,), (right_dim,)), ((), ())), pre...]
    pallas_call x0 -> x2, Pallas kernels: none -> 14.7 us  [the longest x1 8.62 us: hidden_layer(): pl.pallas_call(hidden_kernel, grid=(width // tile,), in_specs=[pl.BlockSp...]
    unnamed x10 -> x17, local copies, waits for them, and re-layouts: 0.03 us -> 7.47 us
  transfers between devices with their start and end apart: 9 -> 17, of which waited for: 4 -> 7; matrix products, arithmetic and copies ran while one was open for 9% -> 5% of each run, Pallas kernels for 0% -> 0%
where the time goes in v1:
time: 198 us; the launch traced here: 197 us
  starting transfers between devices  94.2 us (48%)
  waiting for transfers between devices  68.1 us (34%)
  Pallas kernels  14.7 us (7%)
  local copies, waits for them, and re-layouts  12.4 us (6%)
  other arithmetic  4.98 us (3%)
    all_to_all x1, waiting for transfers between devices, shards(): lax.all_to_all(jnp.broadcast_to(came[None], (parts, 2, count, block)), 't...  16.5 us
    all_to_all x1, starting transfers between devices, shards(): came = lax.all_to_all(sent, 'expert', 0, 0, tiled=True)  15.7 us
    ppermute x1, waiting for transfers between devices, shards(): lax.ppermute(second0, 'dp', ACROSS)  13.2 us
    ppermute x1, waiting for transfers between devices, shards(): rows3 = lax.ppermute(rows[3 * halves:], 'dp', DIAGONAL)  11.3 us
    all_to_all x1, waiting for transfers between devices, shards(): terms = lax.all_to_all(partial_rows, 'tensor', 0, 0, tiled=True)  10.9 us
    all_to_all x1, starting transfers between devices, shards(): lax.all_to_all(row_grads.reshape(experts, capacity, block), 'expert', 0,...  10.9 us
    pallas_call x1, Pallas kernels, hidden_layer(): pl.pallas_call(hidden_kernel, grid=(width // tile,), in_specs=[pl.BlockSp...  8.62 us
    ppermute x1, starting transfers between devices, shards(): acts1 = lax.ppermute(acts0, 'dp', BESIDE)  8.53 us
  transfers between devices with their start and end apart: 17, of which 7 were waited for; matrix products, arithmetic and copies ran while one was open for 5% of the time, Pallas kernels for 0%

profile of v1, /device:TPU:1, one launch (start us, length us, event | category | flops | bytes accessed | tf_op | source)
XLA Modules:
  0.0 196.7 jit_solution(15346732079844895667)
XLA Ops:
  3.7 15.7 %all-to-all-start = ((bf16[16,32,256]{2,1,0:T(8,128)(2,1)}), bf16[16,32,256]{2,1,0:T(8,128)(2,1)S(1)}, u32[]{:S(2)}, u32[]{:S(2)}) async-start(bf16[16,32,256]{2,1,0:T(8,128)(2,1)} %pad_maximum_fusion), calls=%async_computation | async-start | bytes 524288 | tf_op jit(solution)/shard_map/all_to_all | solution.py:163
  19.5 3.1 %collective-permute-start.1 = (bf16[512,1024]{1,0:T(8,128)(2,1)}, bf16[512,1024]{1,0:T(8,128)(2,1)S(1)}, u32[]{:S(2)}, u32[]{:S(2)}) collective-permute-start(bf16[512,1024]{1,0:T(8,128)(2,1)} %bitcast.20), channel_id=1, source_target_pairs={{0,256},{256,0},{128,384},{384,128},{1,257},{257,1},{129,385},{385... | collective-permute-start | bytes 3145736 | tf_op jit(solution)/shard_map/ppermute | solution.py:171
  22.6 2.2 %collective-permute-start.4 = (bf16[1024,512]{1,0:T(8,128)(2,1)}, bf16[1024,512]{1,0:T(8,128)(2,1)}, u32[]{:S(2)}, u32[]{:S(2)}) collective-permute-start(bf16[1024,512]{1,0:T(8,128)(2,1)} %bitcast.30), channel_id=1, source_target_pairs={{0,256},{256,0},{128,384},{384,128},{1,257},{257,1},{129,385},{385... | collective-permute-start | bytes 3145736 | tf_op jit(solution)/shard_map/ppermute | solution.py:171
  24.8 7.8 %all-to-all-done = bf16[16,32,256]{2,1,0:T(8,128)(2,1)S(1)} async-done(((bf16[16,32,256]{2,1,0:T(8,128)(2,1)}), bf16[16,32,256]{2,1,0:T(8,128)(2,1)S(1)}, u32[]{:S(2)}, u32[]{:S(2)}) %all-to-all-start) | async-done | bytes 262176 | tf_op jit(solution)/shard_map/all_to_all | solution.py:163
  34.1 6.8 %all-to-all-start.1 = ((bf16[8,2,256,256]{3,2,1,0:T(8,128)(2,1)}), bf16[8,2,256,256]{3,2,1,0:T(8,128)(2,1)}, u32[]{:S(2)}, u32[]{:S(2)}) async-start(bf16[8,2,256,256]{3,2,1,0:T(8,128)(2,1)} %broadcast_in_dim.27), calls=%async_computation.1 | async-start | bytes 4194304 | tf_op jit(solution)/shard_map/all_to_all | solution.py:166
  40.9 8.4 %collective-permute-start = (bf16[512,1024]{1,0:T(8,128)(2,1)S(1)}, bf16[512,1024]{1,0:T(8,128)(2,1)S(1)}, u32[]{:S(2)}, u32[]{:S(2)}) collective-permute-start(bf16[512,1024]{1,0:T(8,128)(2,1)S(1)} %bitcast.21), channel_id=1, source_target_pairs={{0,128},{128,0},{256,384},{384,256},{1,129},{129,1},{257,385},{385... | collective-permute-start | bytes 3145736 | tf_op jit(solution)/shard_map/ppermute | solution.py:172
  51.3 2.4 %collective-permute-start.2 = (bf16[512,1024]{1,0:T(8,128)(2,1)S(1)}, bf16[512,1024]{1,0:T(8,128)(2,1)S(1)}, u32[]{:S(2)}, u32[]{:S(2)}) collective-permute-start(bf16[512,1024]{1,0:T(8,128)(2,1)S(1)} %collective-permute-done.1.refs_2_), channel_id=1, source_target_pairs={{0,128},{128,0},{256,384},{384,256},{1,129},{129,1},{257,385},{385... | collective-permute-start | bytes 3145736 | tf_op jit(solution)/shard_map/ppermute | solution.py:173
  54.6 13.2 %collective-permute-done.4.refs_6_ = bf16[1024,512]{1,0:T(8,128)(2,1)} collective-permute-done((bf16[1024,512]{1,0:T(8,128)(2,1)}, bf16[1024,512]{1,0:T(8,128)(2,1)}, u32[]{:S(2)}, u32[]{:S(2)}) %collective-permute-start.4) | collective-permute-done | bytes 1048608 | tf_op jit(solution)/shard_map/ppermute | solution.py:171
  67.9 5.2 %collective-permute-start.5 = (bf16[1024,512]{1,0:T(8,128)(2,1)}, bf16[1024,512]{1,0:T(8,128)(2,1)}, u32[]{:S(2)}, u32[]{:S(2)}) collective-permute-start(bf16[1024,512]{1,0:T(8,128)(2,1)} %collective-permute-done.4.refs_6_), channel_id=1, source_target_pairs={{0,128},{128,0},{256,384},{384,256},{1,129},{129,1},{257,385},{385... | collective-permute-start | bytes 3145736 | tf_op jit(solution)/shard_map/ppermute | solution.py:173
  76.0 16.5 %all-to-all-done.1.rows_ref.refs_0_ = bf16[8,2,256,256]{3,2,1,0:T(8,128)(2,1)} async-done(((bf16[8,2,256,256]{3,2,1,0:T(8,128)(2,1)}), bf16[8,2,256,256]{3,2,1,0:T(8,128)(2,1)}, u32[]{:S(2)}, u32[]{:S(2)}) %all-to-all-start.1) | async-done | bytes 2097184 | tf_op jit(solution)/shard_map/all_to_all | solution.py:166
  95.0 8.6 %hidden_layer.1 = (bf16[2,256,1024]{2,1,0:T(8,128)(2,1)S(1)}, bf16[8,256,256]{2,1,0:T(8,128)(2,1)}) custom-call(bf16[8,2,256,256]{3,2,1,0:T(8,128)(2,1)} %all-to-all-done.1.rows_ref.refs_0_, bf16[512,1024]{1,0:T(8,128)(2,1)S(1)} %bitcast.22, bf16[512,1024]{1,0:T(8,128)(2,1)S(1)} %copy-done.5, bf16[512,1024]{1,0:T(8,128)(2,1)S(1)} %copy-done.3, ...), custom_call_target="tpu_custom_call" | custom-call | flops 3221225472 | bytes 13631488 | tf_op jit(solution)/shard_map/hidden_layer/pallas_call | solution.py:76
  103.6 4.4 %all-to-all-start.2 = ((bf16[8,256,256]{2,1,0:T(8,128)(2,1)}), bf16[8,256,256]{2,1,0:T(8,128)(2,1)}, u32[]{:S(2)}, u32[]{:S(2)}) async-start(bf16[8,256,256]{2,1,0:T(8,128)(2,1)} %get-tuple-element.7), calls=%async_computation.2 | async-start | bytes 2097152 | tf_op jit(solution)/shard_map/all_to_all | solution.py:179
  108.0 2.1 %collective-permute-start.10 = (bf16[2,256,1024]{2,1,0:T(8,128)(2,1)S(1)}, bf16[2,256,1024]{2,1,0:T(8,128)(2,1)S(1)}, u32[]{:S(2)}, u32[]{:S(2)}) collective-permute-start(bf16[2,256,1024]{2,1,0:T(8,128)(2,1)S(1)} %get-tuple-element.8.refs_4_), channel_id=1, source_target_pairs={{0,256},{256,0},{128,384},{384,128},{1,257},{257,1},{129,385},{385... | collective-permute-start | bytes 3145736 | tf_op jit(solution)/shard_map/ppermute | solution.py:196
  110.2 10.9 %all-to-all-done.2 = bf16[8,256,256]{2,1,0:T(8,128)(2,1)} async-done(((bf16[8,256,256]{2,1,0:T(8,128)(2,1)}), bf16[8,256,256]{2,1,0:T(8,128)(2,1)}, u32[]{:S(2)}, u32[]{:S(2)}) %all-to-all-start.2) | async-done | bytes 1048608 | tf_op jit(solution)/shard_map/all_to_all | solution.py:179
  123.2 10.9 %all-to-all-start.3 = ((bf16[16,16,256]{2,1,0:T(8,128)(2,1)}), bf16[16,16,256]{2,1,0:T(8,128)(2,1)S(1)}, u32[]{:S(2)}, u32[]{:S(2)}) async-start(bf16[16,16,256]{2,1,0:T(8,128)(2,1)} %bitcast.7), calls=%async_computation.3 | async-start | bytes 262144 | tf_op jit(solution)/shard_map/all_to_all | solution.py:181
  134.0 8.5 %collective-permute-start.9 = (bf16[2,256,1024]{2,1,0:T(8,128)(2,1)S(1)}, bf16[2,256,1024]{2,1,0:T(8,128)(2,1)}, u32[]{:S(2)}, u32[]{:S(2)}) collective-permute-start(bf16[2,256,1024]{2,1,0:T(8,128)(2,1)S(1)} %get-tuple-element.8.refs_4_), channel_id=1, source_target_pairs={{0,128},{128,0},{256,384},{384,256},{1,129},{129,1},{257,385},{385... | collective-permute-start | bytes 3145736 | tf_op jit(solution)/shard_map/ppermute | solution.py:197
  142.6 3.2 %collective-permute-start.11 = (bf16[2,256,1024]{2,1,0:T(8,128)(2,1)S(1)}, bf16[2,256,1024]{2,1,0:T(8,128)(2,1)}, u32[]{:S(2)}, u32[]{:S(2)}) collective-permute-start(bf16[2,256,1024]{2,1,0:T(8,128)(2,1)S(1)} %collective-permute-done.10.refs_6_), channel_id=1, source_target_pairs={{0,128},{128,0},{256,384},{384,256},{1,129},{129,1},{257,385},{385... | collective-permute-start | bytes 3145736 | tf_op jit(solution)/shard_map/ppermute | solution.py:198
  147.2 7.3 %all-to-all-start.4 = ((bf16[8,128,256]{2,1,0:T(8,128)(2,1)}), bf16[8,128,256]{2,1,0:T(8,128)(2,1)}, u32[]{:S(2)}, u32[]{:S(2)}) async-start(bf16[8,128,256]{2,1,0:T(8,128)(2,1)} %broadcast_in_dim.28), calls=%async_computation.4 | async-start | bytes 1048576 | tf_op jit(solution)/shard_map/all_to_all | solution.py:185
  154.5 2.5 %fusion.8 = (bf16[2,2,256,256]{3,2,1,0:T(8,128)(2,1)}, bf16[2,2,256,256]{3,2,1,0:T(8,128)(2,1)}, bf16[2,2,256,256]{3,2,1,0:T(8,128)(2,1)}) fusion(bf16[8,2,256,256]{3,2,1,0:T(8,128)(2,1)} %all-to-all-done.1.rows_ref.refs_0_), kind=kLoop, calls=%fused_computation.17 | loop fusion | bytes 3145728 | tf_op jit(solution)/shard_map/slice | solution.py:195
  157.0 6.5 %collective-permute-start.6 = (bf16[2,2,256,256]{3,2,1,0:T(8,128)(2,1)}, bf16[2,2,256,256]{3,2,1,0:T(8,128)(2,1)S(1)}, u32[]{:S(2)}, u32[]{:S(2)}) collective-permute-start(bf16[2,2,256,256]{3,2,1,0:T(8,128)(2,1)} %get-tuple-element.13), channel_id=1, source_target_pairs={{0,128},{128,0},{256,384},{384,256},{1,129},{129,1},{257,385},{385... | collective-permute-start | bytes 1572872 | tf_op jit(solution)/shard_map/ppermute | solution.py:193
  165.7 3.4 %collective-permute-start.8 = (bf16[2,2,256,256]{3,2,1,0:T(8,128)(2,1)}, bf16[2,2,256,256]{3,2,1,0:T(8,128)(2,1)}, u32[]{:S(2)}, u32[]{:S(2)}) collective-permute-start(bf16[2,2,256,256]{3,2,1,0:T(8,128)(2,1)} %get-tuple-element.11), channel_id=1, source_target_pairs={{0,384},{384,0},{128,256},{256,128},{1,385},{385,1},{129,257},{257... | collective-permute-start | bytes 1572872 | tf_op jit(solution)/shard_map/ppermute | solution.py:195
  171.4 7.9 %collective-permute-done.7.refs_2_ = bf16[2,2,256,256]{3,2,1,0:T(8,128)(2,1)} collective-permute-done((bf16[2,2,256,256]{3,2,1,0:T(8,128)(2,1)}, bf16[2,2,256,256]{3,2,1,0:T(8,128)(2,1)}, u32[]{:S(2)}, u32[]{:S(2)}) %collective-permute-start.7) | collective-permute-done | bytes 524320 | tf_op jit(solution)/shard_map/ppermute | solution.py:194
  179.3 11.3 %collective-permute-done.8.refs_3_ = bf16[2,2,256,256]{3,2,1,0:T(8,128)(2,1)} collective-permute-done((bf16[2,2,256,256]{3,2,1,0:T(8,128)(2,1)}, bf16[2,2,256,256]{3,2,1,0:T(8,128)(2,1)}, u32[]{:S(2)}, u32[]{:S(2)}) %collective-permute-start.8) | collective-permute-done | bytes 524320 | tf_op jit(solution)/shard_map/ppermute | solution.py:195
  190.7 6.0 %weight_grads.1 = (bf16[512,1024]{1,0:T(8,128)(2,1)}, bf16[1024,512]{1,0:T(8,128)(2,1)}) custom-call(bf16[8,2,256,256]{3,2,1,0:T(8,128)(2,1)} %all-to-all-done.1.rows_ref.refs_0_, bf16[2,2,256,256]{3,2,1,0:T(8,128)(2,1)S(1)} %collective-permute-done.6.refs_1_, bf16[2,2,256,256]{3,2,1,0:T(8,128)(2,1)} %collective-permute-done.7.refs_2_, ...), custom_call_target="tpu_custom_call" | custom-call | flops 2147483648 | bytes 8388608 | tf_op jit(solution)/shard_map/weight_grads/pallas_call | solution.py:117
  (41 shorter events, 20.7 us)
Async XLA Ops:
  0.6 1.1 copy-start
  3.7 28.9 %all-to-all-start = ((bf16[16,32,256]{2,1,0:T(8,128)(2,1)}), bf16[16,32,256]{2,1,0:T(8,128)(2,1)S(1)}, u32[]{:S(2)}, u32[]{:S(2)}) async-start(bf16[16,32,256]{2,1,0:T(8,128)(2,1)} %pad_maximum_fusion), calls=%async_computation | async-start | bytes 524288 | tf_op jit(solution)/shard_map/all_to_all | solution.py:163
  19.5 31.8 %collective-permute-start.1 = (bf16[512,1024]{1,0:T(8,128)(2,1)}, bf16[512,1024]{1,0:T(8,128)(2,1)S(1)}, u32[]{:S(2)}, u32[]{:S(2)}) collective-permute-start(bf16[512,1024]{1,0:T(8,128)(2,1)} %bitcast.20), channel_id=1, source_target_pairs={{0,256},{256,0},{128,384},{384,128},{1,257},{257,1},{129,385},{385... | collective-permute-start | bytes 3145736 | tf_op jit(solution)/shard_map/ppermute | solution.py:171
  22.6 45.3 %collective-permute-start.4 = (bf16[1024,512]{1,0:T(8,128)(2,1)}, bf16[1024,512]{1,0:T(8,128)(2,1)}, u32[]{:S(2)}, u32[]{:S(2)}) collective-permute-start(bf16[1024,512]{1,0:T(8,128)(2,1)} %bitcast.30), channel_id=1, source_target_pairs={{0,256},{256,0},{128,384},{384,128},{1,257},{257,1},{129,385},{385... | collective-permute-start | bytes 3145736 | tf_op jit(solution)/shard_map/ppermute | solution.py:171
  34.1 6.8 %copy-start.1 = (bf16[1,512,1024]{2,1,0:T(8,128)(2,1)S(1)}, bf16[1,512,1024]{2,1,0:T(8,128)(2,1)}, u32[]{:S(2)}) copy-start(bf16[1,512,1024]{2,1,0:T(8,128)(2,1)} %param.12) | copy-start | bytes 3145732
  34.1 58.4 %all-to-all-start.1 = ((bf16[8,2,256,256]{3,2,1,0:T(8,128)(2,1)}), bf16[8,2,256,256]{3,2,1,0:T(8,128)(2,1)}, u32[]{:S(2)}, u32[]{:S(2)}) async-start(bf16[8,2,256,256]{3,2,1,0:T(8,128)(2,1)} %broadcast_in_dim.27), calls=%async_computation.1 | async-start | bytes 4194304 | tf_op jit(solution)/shard_map/all_to_all | solution.py:166
  40.9 32.2 %collective-permute-start = (bf16[512,1024]{1,0:T(8,128)(2,1)S(1)}, bf16[512,1024]{1,0:T(8,128)(2,1)S(1)}, u32[]{:S(2)}, u32[]{:S(2)}) collective-permute-start(bf16[512,1024]{1,0:T(8,128)(2,1)S(1)} %bitcast.21), channel_id=1, source_target_pairs={{0,128},{128,0},{256,384},{384,256},{1,129},{129,1},{257,385},{385... | collective-permute-start | bytes 3145736 | tf_op jit(solution)/shard_map/ppermute | solution.py:172
  49.3 24.8 %collective-permute-start.3 = (bf16[1024,512]{1,0:T(8,128)(2,1)}, bf16[1024,512]{1,0:T(8,128)(2,1)S(1)}, u32[]{:S(2)}, u32[]{:S(2)}) collective-permute-start(bf16[1024,512]{1,0:T(8,128)(2,1)} %bitcast.31), channel_id=1, source_target_pairs={{0,128},{128,0},{256,384},{384,256},{1,129},{129,1},{257,385},{385... | collective-permute-start | bytes 3145736 | tf_op jit(solution)/shard_map/ppermute | solution.py:172
  51.3 22.8 %collective-permute-start.2 = (bf16[512,1024]{1,0:T(8,128)(2,1)S(1)}, bf16[512,1024]{1,0:T(8,128)(2,1)S(1)}, u32[]{:S(2)}, u32[]{:S(2)}) collective-permute-start(bf16[512,1024]{1,0:T(8,128)(2,1)S(1)} %collective-permute-done.1.refs_2_), channel_id=1, source_target_pairs={{0,128},{128,0},{256,384},{384,256},{1,129},{129,1},{257,385},{385... | collective-permute-start | bytes 3145736 | tf_op jit(solution)/shard_map/ppermute | solution.py:173
  53.7 1.0 copy-start.2
  67.9 8.2 %collective-permute-start.5 = (bf16[1024,512]{1,0:T(8,128)(2,1)}, bf16[1024,512]{1,0:T(8,128)(2,1)}, u32[]{:S(2)}, u32[]{:S(2)}) collective-permute-start(bf16[1024,512]{1,0:T(8,128)(2,1)} %collective-permute-done.4.refs_6_), channel_id=1, source_target_pairs={{0,128},{128,0},{256,384},{384,256},{1,129},{129,1},{257,385},{385... | collective-permute-start | bytes 3145736 | tf_op jit(solution)/shard_map/ppermute | solution.py:173
  73.1 1.0 copy-start.4
  75.1 1.0 copy-start.7
  92.5 1.2 copy-start.3
  93.8 1.2 copy-start.5
  103.6 17.5 %all-to-all-start.2 = ((bf16[8,256,256]{2,1,0:T(8,128)(2,1)}), bf16[8,256,256]{2,1,0:T(8,128)(2,1)}, u32[]{:S(2)}, u32[]{:S(2)}) async-start(bf16[8,256,256]{2,1,0:T(8,128)(2,1)} %get-tuple-element.7), calls=%async_computation.2 | async-start | bytes 2097152 | tf_op jit(solution)/shard_map/all_to_all | solution.py:179
  108.0 34.5 %collective-permute-start.10 = (bf16[2,256,1024]{2,1,0:T(8,128)(2,1)S(1)}, bf16[2,256,1024]{2,1,0:T(8,128)(2,1)S(1)}, u32[]{:S(2)}, u32[]{:S(2)}) collective-permute-start(bf16[2,256,1024]{2,1,0:T(8,128)(2,1)S(1)} %get-tuple-element.8.refs_4_), channel_id=1, source_target_pairs={{0,256},{256,0},{128,384},{384,128},{1,257},{257,1},{129,385},{385... | collective-permute-start | bytes 3145736 | tf_op jit(solution)/shard_map/ppermute | solution.py:196
  123.2 22.9 %all-to-all-start.3 = ((bf16[16,16,256]{2,1,0:T(8,128)(2,1)}), bf16[16,16,256]{2,1,0:T(8,128)(2,1)S(1)}, u32[]{:S(2)}, u32[]{:S(2)}) async-start(bf16[16,16,256]{2,1,0:T(8,128)(2,1)} %bitcast.7), calls=%async_computation.3 | async-start | bytes 262144 | tf_op jit(solution)/shard_map/all_to_all | solution.py:181
  134.0 56.7 %collective-permute-start.9 = (bf16[2,256,1024]{2,1,0:T(8,128)(2,1)S(1)}, bf16[2,256,1024]{2,1,0:T(8,128)(2,1)}, u32[]{:S(2)}, u32[]{:S(2)}) collective-permute-start(bf16[2,256,1024]{2,1,0:T(8,128)(2,1)S(1)} %get-tuple-element.8.refs_4_), channel_id=1, source_target_pairs={{0,128},{128,0},{256,384},{384,256},{1,129},{129,1},{257,385},{385... | collective-permute-start | bytes 3145736 | tf_op jit(solution)/shard_map/ppermute | solution.py:197
  142.6 48.1 %collective-permute-start.11 = (bf16[2,256,1024]{2,1,0:T(8,128)(2,1)S(1)}, bf16[2,256,1024]{2,1,0:T(8,128)(2,1)}, u32[]{:S(2)}, u32[]{:S(2)}) collective-permute-start(bf16[2,256,1024]{2,1,0:T(8,128)(2,1)S(1)} %collective-permute-done.10.refs_6_), channel_id=1, source_target_pairs={{0,128},{128,0},{256,384},{384,256},{1,129},{129,1},{257,385},{385... | collective-permute-start | bytes 3145736 | tf_op jit(solution)/shard_map/ppermute | solution.py:198
  147.2 21.9 %all-to-all-start.4 = ((bf16[8,128,256]{2,1,0:T(8,128)(2,1)}), bf16[8,128,256]{2,1,0:T(8,128)(2,1)}, u32[]{:S(2)}, u32[]{:S(2)}) async-start(bf16[8,128,256]{2,1,0:T(8,128)(2,1)} %broadcast_in_dim.28), calls=%async_computation.4 | async-start | bytes 1048576 | tf_op jit(solution)/shard_map/all_to_all | solution.py:185
  157.0 14.4 %collective-permute-start.6 = (bf16[2,2,256,256]{3,2,1,0:T(8,128)(2,1)}, bf16[2,2,256,256]{3,2,1,0:T(8,128)(2,1)S(1)}, u32[]{:S(2)}, u32[]{:S(2)}) collective-permute-start(bf16[2,2,256,256]{3,2,1,0:T(8,128)(2,1)} %get-tuple-element.13), channel_id=1, source_target_pairs={{0,128},{128,0},{256,384},{384,256},{1,129},{129,1},{257,385},{385... | collective-permute-start | bytes 1572872 | tf_op jit(solution)/shard_map/ppermute | solution.py:193
  163.6 15.8 %collective-permute-start.7 = (bf16[2,2,256,256]{3,2,1,0:T(8,128)(2,1)}, bf16[2,2,256,256]{3,2,1,0:T(8,128)(2,1)}, u32[]{:S(2)}, u32[]{:S(2)}) collective-permute-start(bf16[2,2,256,256]{3,2,1,0:T(8,128)(2,1)} %get-tuple-element.12), channel_id=1, source_target_pairs={{0,256},{256,0},{128,384},{384,128},{1,257},{257,1},{129,385},{385... | collective-permute-start | bytes 1572872 | tf_op jit(solution)/shard_map/ppermute | solution.py:194
  165.7 25.0 %collective-permute-start.8 = (bf16[2,2,256,256]{3,2,1,0:T(8,128)(2,1)}, bf16[2,2,256,256]{3,2,1,0:T(8,128)(2,1)}, u32[]{:S(2)}, u32[]{:S(2)}) collective-permute-start(bf16[2,2,256,256]{3,2,1,0:T(8,128)(2,1)} %get-tuple-element.11), channel_id=1, source_target_pairs={{0,384},{384,0},{128,256},{256,128},{1,385},{385,1},{129,257},{257... | collective-permute-start | bytes 1572872 | tf_op jit(solution)/shard_map/ppermute | solution.py:195
  (1 other events, 1.0 us)

commit v2 on v1

v2 whole, which is shorter than its diff:
```python
import jax
import jax.numpy as jnp
from jax import lax
from jax.experimental import pallas as pl
from jax.experimental.pallas import tpu as pltpu
from jax.sharding import PartitionSpec as P

ACROSS = [(0, 2), (2, 0), (1, 3), (3, 1)]
DIAGONAL = [(0, 3), (3, 0), (1, 2), (2, 1)]
BESIDE = [(0, 1), (1, 0), (2, 3), (3, 2)]
TILE = 1024
VMEM_BYTES = 24 * 1024 * 1024


def gelu_parts(preact):
    normal_cdf = 0.5 * (1.0 + lax.erf(preact * 0.7071067811865476))
    density = jnp.exp(-0.5 * preact * preact) * 0.3989422804014327
    return (preact * normal_cdf, normal_cdf + preact * density)


def route_table(routes, slots, experts_count, capacity):
    position = jnp.where(slots < capacity, routes * capacity + slots, -1)
    targets = lax.broadcasted_iota(jnp.int32, (experts_count * capacity, routes.shape[0]), 0)
    return (targets == position[None, :]).astype(jnp.bfloat16)


def dot(left, right, left_dim, right_dim):
    return lax.dot_general(
        left,
        right,
        (((left_dim,), (right_dim,)), ((), ())),
        preferred_element_type=jnp.float32,
    )


def hidden_kernel(place_ref, rows_ref, *refs):
    first, second = refs[0:4], refs[4:8]
    acts_ref, sent_ref, total = refs[8:11]
    step, steps = pl.program_id(0), pl.num_programs(0)
    block = sent_ref.shape[2]
    halves = first[0].shape[0] // block

    preact = sum(dot(rows_ref[k, 0], first[k][...], 1, 0) for k in range(4))
    grad_hidden = sum(dot(rows_ref[k, 1], second[k][...], 1, 1) for k in range(4))
    value, slope = gelu_parts(preact)
    grad_pre = (grad_hidden * slope).astype(jnp.bfloat16)
    acts_ref[0] = value.astype(jnp.bfloat16)
    acts_ref[1] = grad_pre

    @pl.when(step == 0)
    def _():
        total[...] = jnp.zeros_like(total)

    for t in range(4 * halves):
        weight = first[t // halves][pl.ds((t % halves) * block, block), :]
        total[t] += dot(grad_pre, weight, 1, 1)

    @pl.when(step == steps - 1)
    def _():
        for t in range(4 * halves):
            sent_ref[place_ref[t]] = total[t].astype(jnp.bfloat16)


def hidden_layer(places, rows, first, second):
    _, _, count, depth = rows.shape
    width = first[0].shape[1]
    parts = places.shape[0]
    block = 4 * depth // parts
    spec = pltpu.PrefetchScalarGridSpec(
        num_scalar_prefetch=1,
        grid=(width // TILE,),
        in_specs=[pl.BlockSpec(rows.shape, lambda j, _: (0, 0, 0, 0))]
        + [pl.BlockSpec((depth, TILE), lambda j, _: (0, j))] * 4
        + [pl.BlockSpec((TILE, depth), lambda j, _: (j, 0))] * 4,
        out_specs=[
            pl.BlockSpec((2, count, TILE), lambda j, _: (0, 0, j)),
            pl.BlockSpec((parts, count, block), lambda j, _: (0, 0, 0)),
        ],
        scratch_shapes=[pltpu.VMEM((parts, count, block), jnp.float32)],
    )
    return pl.pallas_call(
        hidden_kernel,
        grid_spec=spec,
        out_shape=[
            jax.ShapeDtypeStruct((2, count, width), jnp.bfloat16),
            jax.ShapeDtypeStruct((parts, count, block), jnp.bfloat16),
        ],
        compiler_params=pltpu.CompilerParams(vmem_limit_bytes=VMEM_BYTES),
        cost_estimate=pl.CostEstimate(
            flops=24 * count * depth * width,
            bytes_accessed=24 * count * depth * 4,
            transcendentals=2 * count * width,
        ),
        name="hidden_layer",
    )(places, rows, *first, *second)


def total_kernel(terms_ref, out_ref):
    out_ref[...] = jnp.sum(terms_ref[...].astype(jnp.float32), axis=0).astype(jnp.bfloat16)


def total_rows(terms):
    parts, count, block = terms.shape
    tile = count // 2
    return pl.pallas_call(
        total_kernel,
        grid=(count // tile,),
        in_specs=[pl.BlockSpec((parts, tile, block), lambda j: (0, j, 0))],
        out_specs=pl.BlockSpec((tile, block), lambda j: (j, 0)),
        out_shape=jax.ShapeDtypeStruct((count, block), jnp.bfloat16),
        name="total_rows",
    )(terms)


def join_kernel(pieces_ref, out_ref):
    parts, _, block = pieces_ref.shape
    for t in range(parts):
        out_ref[:, pl.ds(t * block, block)] = pieces_ref[t]


def join_columns(pieces):
    parts, group, block = pieces.shape
    return pl.pallas_call(
        join_kernel,
        out_shape=jax.ShapeDtypeStruct((group, parts * block), jnp.bfloat16),
        name="join_columns",
    )(pieces)


def weights_kernel(*refs):
    rows, acts = refs[0:4], refs[4:8]
    first_ref, second_ref = refs[8:10]
    first_ref[...] = sum(dot(rows[k][0], acts[k][1], 0, 0) for k in range(4)).astype(jnp.bfloat16)
    second_ref[...] = sum(dot(acts[k][0], rows[k][1], 0, 0) for k in range(4)).astype(jnp.bfloat16)


def weight_grads(rows, acts):
    _, _, count, depth = rows[0].shape
    width = acts[0].shape[2]
    return pl.pallas_call(
        weights_kernel,
        grid=(width // TILE,),
        in_specs=[pl.BlockSpec((None, 2, count, depth), lambda j: (0, 0, 0, 0))] * 4
        + [pl.BlockSpec((2, count, TILE), lambda j: (0, 0, j))] * 4,
        out_specs=[
            pl.BlockSpec((depth, TILE), lambda j: (0, j)),
            pl.BlockSpec((TILE, depth), lambda j: (j, 0)),
        ],
        out_shape=[
            jax.ShapeDtypeStruct((depth, width), jnp.bfloat16),
            jax.ShapeDtypeStruct((width, depth), jnp.bfloat16),
        ],
        compiler_params=pltpu.CompilerParams(vmem_limit_bytes=VMEM_BYTES),
        cost_estimate=pl.CostEstimate(
            flops=16 * count * depth * width,
            bytes_accessed=8 * 1024 * 1024,
            transcendentals=0,
        ),
        name="weight_grads",
    )(*rows, *acts)


def shards(tokens, routes, slots, gate, cotangent, w_in, w_out):
    experts = lax.axis_size("expert")
    parts = lax.axis_size("tensor")
    ring = lax.axis_size("dp")
    group, model_width = tokens.shape
    capacity = 2 * group // experts
    count = experts * capacity
    block = model_width // parts
    depth = model_width // ring
    halves = parts // ring
    replica = lax.axis_index("dp").astype(jnp.int32)
    y = lax.axis_index("tensor").astype(jnp.int32) % ring
    rings = [[i * ring + j for j in range(ring)] for i in range(halves)]

    start = (replica ^ y) * depth
    own_tokens = lax.dynamic_slice_in_dim(tokens, start, depth, 1)
    own_cotangent = lax.dynamic_slice_in_dim(cotangent, start, depth, 1)
    scaled = (own_cotangent.astype(jnp.float32) * gate[:, None]).astype(jnp.bfloat16)
    table = route_table(routes, slots, experts, capacity)
    sent_tokens = dot(table, own_tokens, 1, 0).astype(jnp.bfloat16)
    sent_grads = dot(table, scaled, 1, 0).astype(jnp.bfloat16)
    sent = jnp.concatenate(
        [
            sent_tokens.reshape(experts, capacity, depth),
            sent_grads.reshape(experts, capacity, depth),
        ],
        axis=1,
    )
    came = lax.all_to_all(sent, "expert", 0, 0, tiled=True)
    came = came.reshape(experts, 2, capacity, depth).transpose(1, 0, 2, 3)
    copies = jnp.broadcast_to(came.reshape(1, 2, count, depth), (ring, 2, count, depth))
    rows = lax.all_to_all(copies, "tensor", 0, 0, axis_index_groups=rings, tiled=True)

    first0, second0 = w_in[0], w_out[0]
    first2, second2 = lax.ppermute(first0, "dp", ACROSS), lax.ppermute(second0, "dp", ACROSS)
    first1, second1 = lax.ppermute(first0, "dp", BESIDE), lax.ppermute(second0, "dp", BESIDE)
    first3, second3 = lax.ppermute(first2, "dp", BESIDE), lax.ppermute(second2, "dp", BESIDE)

    order = jnp.arange(parts, dtype=jnp.int32)
    places = ((order // halves) ^ replica) * halves + order % halves
    acts0, partial_rows = hidden_layer(
        places, rows, (first0, first1, first2, first3), (second0, second1, second2, second3)
    )

    rows1 = lax.ppermute(rows[1:2], "dp", BESIDE)
    rows2 = lax.ppermute(rows[2:3], "dp", ACROSS)
    rows3 = lax.ppermute(rows[3:4], "dp", DIAGONAL)
    acts1 = lax.ppermute(acts0, "dp", BESIDE)
    acts2 = lax.ppermute(acts0, "dp", ACROSS)
    partial_rows, rows2 = lax.optimization_barrier((partial_rows, rows2))
    terms = lax.all_to_all(partial_rows, "tensor", 0, 0, tiled=True)
    row_grads = total_rows(terms)
    row_grads, rows1, acts1 = lax.optimization_barrier((row_grads, rows1, acts1))
    returned = lax.all_to_all(
        row_grads.reshape(experts, capacity, block), "expert", 0, 0, tiled=True
    ).reshape(count, block)
    own_grads = dot(table, returned, 0, 0).astype(jnp.bfloat16)
    own_grads, acts2, rows3 = lax.optimization_barrier((own_grads, acts2, rows3))
    acts3 = lax.ppermute(acts2, "dp", BESIDE)
    pieces = lax.all_to_all(
        jnp.broadcast_to(own_grads[None], (parts, group, block)), "tensor", 0, 0, tiled=True
    )
    grad_first, grad_second = weight_grads((rows, rows1, rows2, rows3), (acts0, acts1, acts2, acts3))
    pieces, grad_first, grad_second = lax.optimization_barrier((pieces, grad_first, grad_second))
    grad_tokens = join_columns(pieces)
    return grad_tokens, grad_first[None], grad_second[None]


def solution(mesh):
    return jax.shard_map(
        shards,
        mesh=mesh,
        in_specs=(
            P(("dp", "expert"), None),
            P(("dp", "expert")),
            P(("dp", "expert")),
            P(("dp", "expert")),
            P(("dp", "expert"), None),
            P("expert", "dp", "tensor"),
            P("expert", "tensor", "dp"),
        ),
        out_specs=(
            P(("dp", "expert"), None),
            P("expert", "dp", "tensor"),
            P("expert", "tensor", "dp"),
        ),
        check_vma=False,
    )
```

time: 198 us -> 166 us (0.84)
  the two profiles are of different devices: /device:TPU:1 before, /device:TPU:32 now
where the time goes in v2:
time: 166 us; the launch traced here: 165 us
  starting transfers between devices  71.6 us (43%)
  waiting for transfers between devices  67.9 us (41%)
  Pallas kernels  17 us (10%)
  local copies, waits for them, and re-layouts  4.73 us (3%)
    all_to_all x1, waiting for transfers between devices, shards(): came = lax.all_to_all(sent, 'expert', 0, 0, tiled=True)  22.4 us
    all_to_all x1, starting transfers between devices, shards(): came = lax.all_to_all(sent, 'expert', 0, 0, tiled=True)  15.2 us
    all_to_all x1, starting transfers between devices, shards(): lax.all_to_all(row_grads.reshape(experts, capacity, block), 'expert', 0,...  12.4 us
    all_to_all x1, waiting for transfers between devices, shards(): terms = lax.all_to_all(partial_rows, 'tensor', 0, 0, tiled=True)  12.1 us
    all_to_all x1, waiting for transfers between devices, shards(): lax.all_to_all(row_grads.reshape(experts, capacity, block), 'expert', 0,...  10.8 us
    ppermute x1, waiting for transfers between devices, shards(): lax.ppermute(second0, 'dp', ACROSS)  8.49 us
    pallas_call x1, Pallas kernels, hidden_layer(): pl.pallas_call(hidden_kernel, grid_spec=spec, out_shape=[jax.ShapeDtypeSt...  7.4 us
    all_to_all x1, starting transfers between devices, shards(): lax.all_to_all(jnp.broadcast_to(own_grads[None], (parts, group, block)),...  7.26 us
  transfers between devices with their start and end apart: 17, of which 7 were waited for; matrix products, arithmetic and copies ran while one was open for 2% of the time, Pallas kernels for 9%

profile of v2, /device:TPU:32, one launch (start us, length us, event | category | flops | bytes accessed | tf_op | source)
XLA Modules:
  0.0 165.3 jit_solution(18173287009715462640)
XLA Ops:
  4.0 15.2 %all-to-all-start = ((bf16[16,32,512]{2,1,0:T(8,128)(2,1)}), bf16[16,32,512]{2,1,0:T(8,128)(2,1)S(1)}, u32[]{:S(2)}, u32[]{:S(2)}) async-start(bf16[16,32,512]{2,1,0:T(8,128)(2,1)} %pad_maximum_fusion), calls=%async_computation | async-start | bytes 1048576 | tf_op jit(solution)/shard_map/all_to_all | solution.py:191
  19.2 3.4 %collective-permute-start.1 = (bf16[512,1024]{1,0:T(8,128)(2,1)}, bf16[512,1024]{1,0:T(8,128)(2,1)}, u32[]{:S(2)}, u32[]{:S(2)}) collective-permute-start(bf16[512,1024]{1,0:T(8,128)(2,1)} %bitcast.5.refs_0_), channel_id=1, source_target_pairs={{0,256},{256,0},{128,384},{384,128},{1,257},{257,1},{129,385},{385... | collective-permute-start | bytes 3145736 | tf_op jit(solution)/shard_map/ppermute | solution.py:197
  22.6 2.4 %collective-permute-start.4 = (bf16[1024,512]{1,0:T(8,128)(2,1)}, bf16[1024,512]{1,0:T(8,128)(2,1)}, u32[]{:S(2)}, u32[]{:S(2)}) collective-permute-start(bf16[1024,512]{1,0:T(8,128)(2,1)} %bitcast.6.refs_4_), channel_id=1, source_target_pairs={{0,256},{256,0},{128,384},{384,128},{1,257},{257,1},{129,385},{385... | collective-permute-start | bytes 3145736 | tf_op jit(solution)/shard_map/ppermute | solution.py:197
  25.1 22.4 %all-to-all-done = bf16[16,32,512]{2,1,0:T(8,128)(2,1)S(1)} async-done(((bf16[16,32,512]{2,1,0:T(8,128)(2,1)}), bf16[16,32,512]{2,1,0:T(8,128)(2,1)S(1)}, u32[]{:S(2)}, u32[]{:S(2)}) %all-to-all-start) | async-done | bytes 524320 | tf_op jit(solution)/shard_map/all_to_all | solution.py:191
  49.0 4.5 %all-to-all-start.1 = ((bf16[4,2,256,512]{3,2,1,0:T(8,128)(2,1)}), bf16[4,2,256,512]{3,2,1,0:T(8,128)(2,1)S(1)}, u32[]{:S(2)}, u32[]{:S(2)}) async-start(bf16[4,2,256,512]{3,2,1,0:T(8,128)(2,1)} %broadcast_in_dim.27), calls=%async_computation.1 | async-start | bytes 4194304 | tf_op jit(solution)/shard_map/all_to_all | solution.py:194
  53.5 1.9 %collective-permute-start = (bf16[512,1024]{1,0:T(8,128)(2,1)}, bf16[512,1024]{1,0:T(8,128)(2,1)}, u32[]{:S(2)}, u32[]{:S(2)}) collective-permute-start(bf16[512,1024]{1,0:T(8,128)(2,1)} %bitcast.5.refs_0_), channel_id=1, source_target_pairs={{0,128},{128,0},{256,384},{384,256},{1,129},{129,1},{257,385},{385... | collective-permute-start | bytes 3145736 | tf_op jit(solution)/shard_map/ppermute | solution.py:198
  55.4 2.4 %collective-permute-start.3 = (bf16[1024,512]{1,0:T(8,128)(2,1)}, bf16[1024,512]{1,0:T(8,128)(2,1)}, u32[]{:S(2)}, u32[]{:S(2)}) collective-permute-start(bf16[1024,512]{1,0:T(8,128)(2,1)} %bitcast.6.refs_4_), channel_id=1, source_target_pairs={{0,128},{128,0},{256,384},{384,256},{1,129},{129,1},{257,385},{385... | collective-permute-start | bytes 3145736 | tf_op jit(solution)/shard_map/ppermute | solution.py:198
  57.8 1.9 %collective-permute-start.2 = (bf16[512,1024]{1,0:T(8,128)(2,1)}, bf16[512,1024]{1,0:T(8,128)(2,1)}, u32[]{:S(2)}, u32[]{:S(2)}) collective-permute-start(bf16[512,1024]{1,0:T(8,128)(2,1)} %collective-permute-done.1.refs_2_), channel_id=1, source_target_pairs={{0,128},{128,0},{256,384},{384,256},{1,129},{129,1},{257,385},{385... | collective-permute-start | bytes 3145736 | tf_op jit(solution)/shard_map/ppermute | solution.py:199
  59.7 8.5 %collective-permute-done.4.refs_6_ = bf16[1024,512]{1,0:T(8,128)(2,1)} collective-permute-done((bf16[1024,512]{1,0:T(8,128)(2,1)}, bf16[1024,512]{1,0:T(8,128)(2,1)}, u32[]{:S(2)}, u32[]{:S(2)}) %collective-permute-start.4) | collective-permute-done | bytes 1048608 | tf_op jit(solution)/shard_map/ppermute | solution.py:197
  68.2 1.9 %collective-permute-start.5 = (bf16[1024,512]{1,0:T(8,128)(2,1)}, bf16[1024,512]{1,0:T(8,128)(2,1)}, u32[]{:S(2)}, u32[]{:S(2)}) collective-permute-start(bf16[1024,512]{1,0:T(8,128)(2,1)} %collective-permute-done.4.refs_6_), channel_id=1, source_target_pairs={{0,128},{128,0},{256,384},{384,256},{1,129},{129,1},{257,385},{385... | collective-permute-start | bytes 3145736 | tf_op jit(solution)/shard_map/ppermute | solution.py:199
  70.1 5.6 %all-to-all-done.1.rows_ref.refs_0_ = bf16[4,2,256,512]{3,2,1,0:T(8,128)(2,1)S(1)} async-done(((bf16[4,2,256,512]{3,2,1,0:T(8,128)(2,1)}), bf16[4,2,256,512]{3,2,1,0:T(8,128)(2,1)S(1)}, u32[]{:S(2)}, u32[]{:S(2)}) %all-to-all-start.1) | async-done | bytes 2097184 | tf_op jit(solution)/shard_map/all_to_all | solution.py:194
  76.8 3.4 %collective-permute-start.6 = (bf16[1,2,256,512]{3,2,1,0:T(8,128)(2,1)S(1)}, bf16[1,2,256,512]{3,2,1,0:T(8,128)(2,1)S(1)}, u32[]{:S(2)}, u32[]{:S(2)}) collective-permute-start(bf16[1,2,256,512]{3,2,1,0:T(8,128)(2,1)S(1)} %get-tuple-element.35), channel_id=1, source_target_pairs={{0,256},{256,0},{128,384},{384,128},{1,257},{257,1},{129,385},{385... | collective-permute-start | bytes 1572872 | tf_op jit(solution)/shard_map/ppermute | solution.py:208
  80.3 7.4 %hidden_layer.1 = (bf16[2,256,1024]{2,1,0:T(8,128)(2,1)}, bf16[8,256,256]{2,1,0:T(8,128)(2,1)S(1)}) custom-call(s32[8]{0:T(128)S(1)} %fusion.6.place_ref, bf16[4,2,256,512]{3,2,1,0:T(8,128)(2,1)S(1)} %all-to-all-done.1.rows_ref.refs_0_, bf16[512,1024]{1,0:T(8,128)(2,1)} %bitcast.5.refs_0_, bf16[512,1024]{1,0:T(8,128)(2,1)} %collective-permute-done.refs_1_, ...), custom_call_target="tpu_custom_call" | custom-call | flops 3221225472 | bytes 12582912 | tf_op jit(solution)/shard_map/hidden_layer/pallas_call | solution.py:81
  90.6 4.6 %all-to-all-start.2 = ((bf16[8,256,256]{2,1,0:T(8,128)(2,1)}), bf16[8,256,256]{2,1,0:T(8,128)(2,1)}, u32[]{:S(2)}, u32[]{:S(2)}) async-start(bf16[8,256,256]{2,1,0:T(8,128)(2,1)} %copy-done.1), calls=%async_computation.2 | async-start | bytes 2097152 | tf_op jit(solution)/shard_map/all_to_all | solution.py:213
  95.2 2.1 %collective-permute-start.7 = (bf16[1,2,256,512]{3,2,1,0:T(8,128)(2,1)}, bf16[1,2,256,512]{3,2,1,0:T(8,128)(2,1)}, u32[]{:S(2)}, u32[]{:S(2)}) collective-permute-start(bf16[1,2,256,512]{3,2,1,0:T(8,128)(2,1)} %get-tuple-element.34), channel_id=1, source_target_pairs={{0,128},{128,0},{256,384},{384,256},{1,129},{129,1},{257,385},{385... | collective-permute-start | bytes 1572872 | tf_op jit(solution)/shard_map/ppermute | solution.py:207
  97.3 2.4 %collective-permute-start.9 = (bf16[2,256,1024]{2,1,0:T(8,128)(2,1)}, bf16[2,256,1024]{2,1,0:T(8,128)(2,1)}, u32[]{:S(2)}, u32[]{:S(2)}) collective-permute-start(bf16[2,256,1024]{2,1,0:T(8,128)(2,1)} %get-tuple-element.20.refs_4_), channel_id=1, source_target_pairs={{0,256},{256,0},{128,384},{384,128},{1,257},{257,1},{129,385},{385... | collective-permute-start | bytes 3145736 | tf_op jit(solution)/shard_map/ppermute | solution.py:211
  99.7 12.1 %all-to-all-done.2.terms_ref = bf16[8,256,256]{2,1,0:T(8,128)(2,1)} async-done(((bf16[8,256,256]{2,1,0:T(8,128)(2,1)}), bf16[8,256,256]{2,1,0:T(8,128)(2,1)}, u32[]{:S(2)}, u32[]{:S(2)}) %all-to-all-start.2) | async-done | bytes 1048608 | tf_op jit(solution)/shard_map/all_to_all | solution.py:213
  113.7 12.4 %all-to-all-start.3 = ((bf16[16,16,256]{2,1,0:T(8,128)(2,1)}), bf16[16,16,256]{2,1,0:T(8,128)(2,1)S(1)}, u32[]{:S(2)}, u32[]{:S(2)}) async-start(bf16[16,16,256]{2,1,0:T(8,128)(2,1)} %bitcast.17), calls=%async_computation.3 | async-start | bytes 262144 | tf_op jit(solution)/shard_map/all_to_all | solution.py:216
  128.1 10.8 %all-to-all-done.3 = bf16[16,16,256]{2,1,0:T(8,128)(2,1)S(1)} async-done(((bf16[16,16,256]{2,1,0:T(8,128)(2,1)}), bf16[16,16,256]{2,1,0:T(8,128)(2,1)S(1)}, u32[]{:S(2)}, u32[]{:S(2)}) %all-to-all-start.3) | async-done | bytes 131104 | tf_op jit(solution)/shard_map/all_to_all | solution.py:216
  139.1 3.1 %collective-permute-done.10.refs_3_ = bf16[1,2,256,512]{3,2,1,0:T(8,128)(2,1)} collective-permute-done((bf16[1,2,256,512]{3,2,1,0:T(8,128)(2,1)}, bf16[1,2,256,512]{3,2,1,0:T(8,128)(2,1)}, u32[]{:S(2)}, u32[]{:S(2)}) %collective-permute-start.10) | collective-permute-done | bytes 524320 | tf_op jit(solution)/shard_map/ppermute | solution.py:209
  142.2 1.9 %collective-permute-start.11 = (bf16[2,256,1024]{2,1,0:T(8,128)(2,1)}, bf16[2,256,1024]{2,1,0:T(8,128)(2,1)}, u32[]{:S(2)}, u32[]{:S(2)}) collective-permute-start(bf16[2,256,1024]{2,1,0:T(8,128)(2,1)} %collective-permute-done.9.refs_6_), channel_id=1, source_target_pairs={{0,128},{128,0},{256,384},{384,256},{1,129},{129,1},{257,385},{385... | collective-permute-start | bytes 3145736 | tf_op jit(solution)/shard_map/ppermute | solution.py:221
  144.9 7.3 %all-to-all-start.4 = ((bf16[8,128,256]{2,1,0:T(8,128)(2,1)}), bf16[8,128,256]{2,1,0:T(8,128)(2,1)}, u32[]{:S(2)}, u32[]{:S(2)}) async-start(bf16[8,128,256]{2,1,0:T(8,128)(2,1)} %broadcast_in_dim.28), calls=%async_computation.4 | async-start | bytes 1048576 | tf_op jit(solution)/shard_map/all_to_all | solution.py:222
  152.2 5.8 %weight_grads.1 = (bf16[512,1024]{1,0:T(8,128)(2,1)}, bf16[1024,512]{1,0:T(8,128)(2,1)}) custom-call(bf16[4,2,256,512]{3,2,1,0:T(8,128)(2,1)S(1)} %all-to-all-done.1.rows_ref.refs_0_, bf16[1,2,256,512]{3,2,1,0:T(8,128)(2,1)} %collective-permute-done.7.refs_1_, bf16[1,2,256,512]{3,2,1,0:T(8,128)(2,1)S(1)} %collective-permute-done.6.refs_2_, ...), custom_call_target="tpu_custom_call" | custom-call | flops 2147483648 | bytes 8388608 | tf_op jit(solution)/shard_map/weight_grads/pallas_call | solution.py:140
  158.0 5.4 %all-to-all-done.4.pieces_ref = bf16[8,128,256]{2,1,0:T(8,128)(2,1)} async-done(((bf16[8,128,256]{2,1,0:T(8,128)(2,1)}), bf16[8,128,256]{2,1,0:T(8,128)(2,1)}, u32[]{:S(2)}, u32[]{:S(2)}) %all-to-all-start.4) | async-done | bytes 524320 | tf_op jit(solution)/shard_map/all_to_all | solution.py:222
  (28 shorter events, 15.6 us)
Async XLA Ops:
  0.6 1.1 copy-start
  4.0 43.4 %all-to-all-start = ((bf16[16,32,512]{2,1,0:T(8,128)(2,1)}), bf16[16,32,512]{2,1,0:T(8,128)(2,1)S(1)}, u32[]{:S(2)}, u32[]{:S(2)}) async-start(bf16[16,32,512]{2,1,0:T(8,128)(2,1)} %pad_maximum_fusion), calls=%async_computation | async-start | bytes 1048576 | tf_op jit(solution)/shard_map/all_to_all | solution.py:191
  19.2 38.6 %collective-permute-start.1 = (bf16[512,1024]{1,0:T(8,128)(2,1)}, bf16[512,1024]{1,0:T(8,128)(2,1)}, u32[]{:S(2)}, u32[]{:S(2)}) collective-permute-start(bf16[512,1024]{1,0:T(8,128)(2,1)} %bitcast.5.refs_0_), channel_id=1, source_target_pairs={{0,256},{256,0},{128,384},{384,128},{1,257},{257,1},{129,385},{385... | collective-permute-start | bytes 3145736 | tf_op jit(solution)/shard_map/ppermute | solution.py:197
  22.6 45.6 %collective-permute-start.4 = (bf16[1024,512]{1,0:T(8,128)(2,1)}, bf16[1024,512]{1,0:T(8,128)(2,1)}, u32[]{:S(2)}, u32[]{:S(2)}) collective-permute-start(bf16[1024,512]{1,0:T(8,128)(2,1)} %bitcast.6.refs_4_), channel_id=1, source_target_pairs={{0,256},{256,0},{128,384},{384,128},{1,257},{257,1},{129,385},{385... | collective-permute-start | bytes 3145736 | tf_op jit(solution)/shard_map/ppermute | solution.py:197
  49.0 26.8 %all-to-all-start.1 = ((bf16[4,2,256,512]{3,2,1,0:T(8,128)(2,1)}), bf16[4,2,256,512]{3,2,1,0:T(8,128)(2,1)S(1)}, u32[]{:S(2)}, u32[]{:S(2)}) async-start(bf16[4,2,256,512]{3,2,1,0:T(8,128)(2,1)} %broadcast_in_dim.27), calls=%async_computation.1 | async-start | bytes 4194304 | tf_op jit(solution)/shard_map/all_to_all | solution.py:194
  53.5 26.8 %collective-permute-start = (bf16[512,1024]{1,0:T(8,128)(2,1)}, bf16[512,1024]{1,0:T(8,128)(2,1)}, u32[]{:S(2)}, u32[]{:S(2)}) collective-permute-start(bf16[512,1024]{1,0:T(8,128)(2,1)} %bitcast.5.refs_0_), channel_id=1, source_target_pairs={{0,128},{128,0},{256,384},{384,256},{1,129},{129,1},{257,385},{385... | collective-permute-start | bytes 3145736 | tf_op jit(solution)/shard_map/ppermute | solution.py:198
  55.4 24.9 %collective-permute-start.3 = (bf16[1024,512]{1,0:T(8,128)(2,1)}, bf16[1024,512]{1,0:T(8,128)(2,1)}, u32[]{:S(2)}, u32[]{:S(2)}) collective-permute-start(bf16[1024,512]{1,0:T(8,128)(2,1)} %bitcast.6.refs_4_), channel_id=1, source_target_pairs={{0,128},{128,0},{256,384},{384,256},{1,129},{129,1},{257,385},{385... | collective-permute-start | bytes 3145736 | tf_op jit(solution)/shard_map/ppermute | solution.py:198
  57.8 22.5 %collective-permute-start.2 = (bf16[512,1024]{1,0:T(8,128)(2,1)}, bf16[512,1024]{1,0:T(8,128)(2,1)}, u32[]{:S(2)}, u32[]{:S(2)}) collective-permute-start(bf16[512,1024]{1,0:T(8,128)(2,1)} %collective-permute-done.1.refs_2_), channel_id=1, source_target_pairs={{0,128},{128,0},{256,384},{384,256},{1,129},{129,1},{257,385},{385... | collective-permute-start | bytes 3145736 | tf_op jit(solution)/shard_map/ppermute | solution.py:199
  68.2 12.1 %collective-permute-start.5 = (bf16[1024,512]{1,0:T(8,128)(2,1)}, bf16[1024,512]{1,0:T(8,128)(2,1)}, u32[]{:S(2)}, u32[]{:S(2)}) collective-permute-start(bf16[1024,512]{1,0:T(8,128)(2,1)} %collective-permute-done.4.refs_6_), channel_id=1, source_target_pairs={{0,128},{128,0},{256,384},{384,256},{1,129},{129,1},{257,385},{385... | collective-permute-start | bytes 3145736 | tf_op jit(solution)/shard_map/ppermute | solution.py:199
  76.8 13.8 %collective-permute-start.6 = (bf16[1,2,256,512]{3,2,1,0:T(8,128)(2,1)S(1)}, bf16[1,2,256,512]{3,2,1,0:T(8,128)(2,1)S(1)}, u32[]{:S(2)}, u32[]{:S(2)}) collective-permute-start(bf16[1,2,256,512]{3,2,1,0:T(8,128)(2,1)S(1)} %get-tuple-element.35), channel_id=1, source_target_pairs={{0,256},{256,0},{128,384},{384,128},{1,257},{257,1},{129,385},{385... | collective-permute-start | bytes 1572872 | tf_op jit(solution)/shard_map/ppermute | solution.py:208
  87.7 1.0 copy-start.1
  88.7 25.0 %collective-permute-start.8 = (bf16[2,256,1024]{2,1,0:T(8,128)(2,1)}, bf16[2,256,1024]{2,1,0:T(8,128)(2,1)}, u32[]{:S(2)}, u32[]{:S(2)}) collective-permute-start(bf16[2,256,1024]{2,1,0:T(8,128)(2,1)} %get-tuple-element.20.refs_4_), channel_id=1, source_target_pairs={{0,128},{128,0},{256,384},{384,256},{1,129},{129,1},{257,385},{385... | collective-permute-start | bytes 3145736 | tf_op jit(solution)/shard_map/ppermute | solution.py:210
  90.6 21.2 %all-to-all-start.2 = ((bf16[8,256,256]{2,1,0:T(8,128)(2,1)}), bf16[8,256,256]{2,1,0:T(8,128)(2,1)}, u32[]{:S(2)}, u32[]{:S(2)}) async-start(bf16[8,256,256]{2,1,0:T(8,128)(2,1)} %copy-done.1), calls=%async_computation.2 | async-start | bytes 2097152 | tf_op jit(solution)/shard_map/all_to_all | solution.py:213
  95.2 18.5 %collective-permute-start.7 = (bf16[1,2,256,512]{3,2,1,0:T(8,128)(2,1)}, bf16[1,2,256,512]{3,2,1,0:T(8,128)(2,1)}, u32[]{:S(2)}, u32[]{:S(2)}) collective-permute-start(bf16[1,2,256,512]{3,2,1,0:T(8,128)(2,1)} %get-tuple-element.34), channel_id=1, source_target_pairs={{0,128},{128,0},{256,384},{384,256},{1,129},{129,1},{257,385},{385... | collective-permute-start | bytes 1572872 | tf_op jit(solution)/shard_map/ppermute | solution.py:207
  97.3 44.8 %collective-permute-start.9 = (bf16[2,256,1024]{2,1,0:T(8,128)(2,1)}, bf16[2,256,1024]{2,1,0:T(8,128)(2,1)}, u32[]{:S(2)}, u32[]{:S(2)}) collective-permute-start(bf16[2,256,1024]{2,1,0:T(8,128)(2,1)} %get-tuple-element.20.refs_4_), channel_id=1, source_target_pairs={{0,256},{256,0},{128,384},{384,128},{1,257},{257,1},{129,385},{385... | collective-permute-start | bytes 3145736 | tf_op jit(solution)/shard_map/ppermute | solution.py:211
  113.7 25.2 %all-to-all-start.3 = ((bf16[16,16,256]{2,1,0:T(8,128)(2,1)}), bf16[16,16,256]{2,1,0:T(8,128)(2,1)S(1)}, u32[]{:S(2)}, u32[]{:S(2)}) async-start(bf16[16,16,256]{2,1,0:T(8,128)(2,1)} %bitcast.17), calls=%async_computation.3 | async-start | bytes 262144 | tf_op jit(solution)/shard_map/all_to_all | solution.py:216
  126.1 16.0 %collective-permute-start.10 = (bf16[1,2,256,512]{3,2,1,0:T(8,128)(2,1)}, bf16[1,2,256,512]{3,2,1,0:T(8,128)(2,1)}, u32[]{:S(2)}, u32[]{:S(2)}) collective-permute-start(bf16[1,2,256,512]{3,2,1,0:T(8,128)(2,1)} %get-tuple-element.33), channel_id=1, source_target_pairs={{0,384},{384,0},{128,256},{256,128},{1,385},{385,1},{129,257},{257... | collective-permute-start | bytes 1572872 | tf_op jit(solution)/shard_map/ppermute | solution.py:209
  142.2 10.0 %collective-permute-start.11 = (bf16[2,256,1024]{2,1,0:T(8,128)(2,1)}, bf16[2,256,1024]{2,1,0:T(8,128)(2,1)}, u32[]{:S(2)}, u32[]{:S(2)}) collective-permute-start(bf16[2,256,1024]{2,1,0:T(8,128)(2,1)} %collective-permute-done.9.refs_6_), channel_id=1, source_target_pairs={{0,128},{128,0},{256,384},{384,256},{1,129},{129,1},{257,385},{385... | collective-permute-start | bytes 3145736 | tf_op jit(solution)/shard_map/ppermute | solution.py:221
  144.9 18.5 %all-to-all-start.4 = ((bf16[8,128,256]{2,1,0:T(8,128)(2,1)}), bf16[8,128,256]{2,1,0:T(8,128)(2,1)}, u32[]{:S(2)}, u32[]{:S(2)}) async-start(bf16[8,128,256]{2,1,0:T(8,128)(2,1)} %broadcast_in_dim.28), calls=%async_computation.4 | async-start | bytes 1048576 | tf_op jit(solution)/shard_map/all_to_all | solution.py:222

commit v3 on v2

--- a/solution.py
+++ b/solution.py
@@ -6,7 +6,6 @@
 from jax.sharding import PartitionSpec as P
 
 ACROSS = [(0, 2), (2, 0), (1, 3), (3, 1)]
-DIAGONAL = [(0, 3), (3, 0), (1, 2), (2, 1)]
 BESIDE = [(0, 1), (1, 0), (2, 3), (3, 2)]
 TILE = 1024
 VMEM_BYTES = 24 * 1024 * 1024
@@ -206,18 +205,19 @@
 
     rows1 = lax.ppermute(rows[1:2], "dp", BESIDE)
     rows2 = lax.ppermute(rows[2:3], "dp", ACROSS)
-    rows3 = lax.ppermute(rows[3:4], "dp", DIAGONAL)
+    rows3 = lax.ppermute(lax.ppermute(rows[3:4], "dp", ACROSS), "dp", BESIDE)
     acts1 = lax.ppermute(acts0, "dp", BESIDE)
     acts2 = lax.ppermute(acts0, "dp", ACROSS)
     partial_rows, rows2 = lax.optimization_barrier((partial_rows, rows2))
     terms = lax.all_to_all(partial_rows, "tensor", 0, 0, tiled=True)
     row_grads = total_rows(terms)
-    row_grads, rows1, acts1 = lax.optimization_barrier((row_grads, rows1, acts1))
     returned = lax.all_to_all(
         row_grads.reshape(experts, capacity, block), "expert", 0, 0, tiled=True
     ).reshape(count, block)
     own_grads = dot(table, returned, 0, 0).astype(jnp.bfloat16)
-    own_grads, acts2, rows3 = lax.optimization_barrier((own_grads, acts2, rows3))
+    own_grads, acts1, acts2, rows1, rows3 = lax.optimization_barrier(
+        (own_grads, acts1, acts2, rows1, rows3)
+    )
     acts3 = lax.ppermute(acts2, "dp", BESIDE)
     pieces = lax.all_to_all(
         jnp.broadcast_to(own_grads[None], (parts, group, block)), "tensor", 0, 0, tiled=True

time: 166 us -> 165 us (level)
  the two profiles are of different devices: /device:TPU:32 before, /device:TPU:1 now
where the time goes in v3:
time: 165 us; the launch traced here: 164 us
  starting transfers between devices  99.1 us (60%)
  waiting for transfers between devices  36.7 us (22%)
  Pallas kernels  16.7 us (10%)
  local copies, waits for them, and re-layouts  7 us (4%)
    all_to_all x1, waiting for transfers between devices, shards(): came = lax.all_to_all(sent, 'expert', 0, 0, tiled=True)  17.5 us
    all_to_all x1, starting transfers between devices, shards(): came = lax.all_to_all(sent, 'expert', 0, 0, tiled=True)  15.7 us
    all_to_all x1, starting transfers between devices, shards(): lax.all_to_all(row_grads.reshape(experts, capacity, block), 'expert', 0,...  11.2 us
    ppermute x1, starting transfers between devices, shards(): rows1 = lax.ppermute(rows[1:2], 'dp', BESIDE)  9.62 us
    ppermute x1, starting transfers between devices, shards(): lax.ppermute(first0, 'dp', BESIDE)  9.4 us
    all_to_all x1, starting transfers between devices, shards(): terms = lax.all_to_all(partial_rows, 'tensor', 0, 0, tiled=True)  8.37 us
    all_to_all x1, starting transfers between devices, shards(): lax.all_to_all(jnp.broadcast_to(own_grads[None], (parts, group, block)),...  7.7 us
    pallas_call x1, Pallas kernels, hidden_layer(): pl.pallas_call(hidden_kernel, grid_spec=spec, out_shape=[jax.ShapeDtypeSt...  7.39 us
  transfers between devices with their start and end apart: 18, of which 7 were waited for; matrix products, arithmetic and copies ran while one was open for 2% of the time, Pallas kernels for 9%

profile of v3, /device:TPU:1, one launch (start us, length us, event | category | flops | bytes accessed | tf_op | source)
XLA Modules:
  0.0 163.6 jit_solution(9707552527442275286)
XLA Ops:
  4.0 15.7 %all-to-all-start = ((bf16[16,32,512]{2,1,0:T(8,128)(2,1)}), bf16[16,32,512]{2,1,0:T(8,128)(2,1)S(1)}, u32[]{:S(2)}, u32[]{:S(2)}) async-start(bf16[16,32,512]{2,1,0:T(8,128)(2,1)} %pad_maximum_fusion), calls=%async_computation | async-start | bytes 1048576 | tf_op jit(solution)/shard_map/all_to_all | solution.py:190
  19.7 3.1 %collective-permute-start.1 = (bf16[512,1024]{1,0:T(8,128)(2,1)}, bf16[512,1024]{1,0:T(8,128)(2,1)}, u32[]{:S(2)}, u32[]{:S(2)}) collective-permute-start(bf16[512,1024]{1,0:T(8,128)(2,1)} %bitcast.5.refs_0_), channel_id=1, source_target_pairs={{0,256},{256,0},{128,384},{384,128},{1,257},{257,1},{129,385},{385... | collective-permute-start | bytes 3145736 | tf_op jit(solution)/shard_map/ppermute | solution.py:196
  22.9 2.2 %collective-permute-start.4 = (bf16[1024,512]{1,0:T(8,128)(2,1)}, bf16[1024,512]{1,0:T(8,128)(2,1)}, u32[]{:S(2)}, u32[]{:S(2)}) collective-permute-start(bf16[1024,512]{1,0:T(8,128)(2,1)} %bitcast.6.refs_4_), channel_id=1, source_target_pairs={{0,256},{256,0},{128,384},{384,128},{1,257},{257,1},{129,385},{385... | collective-permute-start | bytes 3145736 | tf_op jit(solution)/shard_map/ppermute | solution.py:196
  25.1 17.5 %all-to-all-done = bf16[16,32,512]{2,1,0:T(8,128)(2,1)S(1)} async-done(((bf16[16,32,512]{2,1,0:T(8,128)(2,1)}), bf16[16,32,512]{2,1,0:T(8,128)(2,1)S(1)}, u32[]{:S(2)}, u32[]{:S(2)}) %all-to-all-start) | async-done | bytes 524320 | tf_op jit(solution)/shard_map/all_to_all | solution.py:190
  44.1 4.2 %all-to-all-start.1 = ((bf16[4,2,256,512]{3,2,1,0:T(8,128)(2,1)}), bf16[4,2,256,512]{3,2,1,0:T(8,128)(2,1)S(1)}, u32[]{:S(2)}, u32[]{:S(2)}) async-start(bf16[4,2,256,512]{3,2,1,0:T(8,128)(2,1)} %broadcast_in_dim.27), calls=%async_computation.1 | async-start | bytes 4194304 | tf_op jit(solution)/shard_map/all_to_all | solution.py:193
  48.3 9.4 %collective-permute-start = (bf16[512,1024]{1,0:T(8,128)(2,1)}, bf16[512,1024]{1,0:T(8,128)(2,1)}, u32[]{:S(2)}, u32[]{:S(2)}) collective-permute-start(bf16[512,1024]{1,0:T(8,128)(2,1)} %bitcast.5.refs_0_), channel_id=1, source_target_pairs={{0,128},{128,0},{256,384},{384,256},{1,129},{129,1},{257,385},{385... | collective-permute-start | bytes 3145736 | tf_op jit(solution)/shard_map/ppermute | solution.py:197
  57.7 1.9 %collective-permute-start.3 = (bf16[1024,512]{1,0:T(8,128)(2,1)}, bf16[1024,512]{1,0:T(8,128)(2,1)}, u32[]{:S(2)}, u32[]{:S(2)}) collective-permute-start(bf16[1024,512]{1,0:T(8,128)(2,1)} %bitcast.6.refs_4_), channel_id=1, source_target_pairs={{0,128},{128,0},{256,384},{384,256},{1,129},{129,1},{257,385},{385... | collective-permute-start | bytes 3145736 | tf_op jit(solution)/shard_map/ppermute | solution.py:197
  59.7 2.4 %collective-permute-start.2 = (bf16[512,1024]{1,0:T(8,128)(2,1)}, bf16[512,1024]{1,0:T(8,128)(2,1)}, u32[]{:S(2)}, u32[]{:S(2)}) collective-permute-start(bf16[512,1024]{1,0:T(8,128)(2,1)} %collective-permute-done.1.refs_2_), channel_id=1, source_target_pairs={{0,128},{128,0},{256,384},{384,256},{1,129},{129,1},{257,385},{385... | collective-permute-start | bytes 3145736 | tf_op jit(solution)/shard_map/ppermute | solution.py:198
  62.1 6.1 %collective-permute-done.4.refs_6_ = bf16[1024,512]{1,0:T(8,128)(2,1)} collective-permute-done((bf16[1024,512]{1,0:T(8,128)(2,1)}, bf16[1024,512]{1,0:T(8,128)(2,1)}, u32[]{:S(2)}, u32[]{:S(2)}) %collective-permute-start.4) | collective-permute-done | bytes 1048608 | tf_op jit(solution)/shard_map/ppermute | solution.py:196
  68.1 3.8 %collective-permute-start.5 = (bf16[1024,512]{1,0:T(8,128)(2,1)}, bf16[1024,512]{1,0:T(8,128)(2,1)}, u32[]{:S(2)}, u32[]{:S(2)}) collective-permute-start(bf16[1024,512]{1,0:T(8,128)(2,1)} %collective-permute-done.4.refs_6_), channel_id=1, source_target_pairs={{0,128},{128,0},{256,384},{384,256},{1,129},{129,1},{257,385},{385... | collective-permute-start | bytes 3145736 | tf_op jit(solution)/shard_map/ppermute | solution.py:198
  73.1 3.1 %collective-permute-start.6 = (bf16[1,2,256,512]{3,2,1,0:T(8,128)(2,1)S(1)}, bf16[1,2,256,512]{3,2,1,0:T(8,128)(2,1)S(1)}, u32[]{:S(2)}, u32[]{:S(2)}) collective-permute-start(bf16[1,2,256,512]{3,2,1,0:T(8,128)(2,1)S(1)} %get-tuple-element.33), channel_id=1, source_target_pairs={{0,256},{256,0},{128,384},{384,128},{1,257},{257,1},{129,385},{385... | collective-permute-start | bytes 1572872 | tf_op jit(solution)/shard_map/ppermute | solution.py:207
  76.2 7.4 %hidden_layer.1 = (bf16[2,256,1024]{2,1,0:T(8,128)(2,1)S(1)}, bf16[8,256,256]{2,1,0:T(8,128)(2,1)S(1)}) custom-call(s32[8]{0:T(128)S(1)} %fusion.6.place_ref, bf16[4,2,256,512]{3,2,1,0:T(8,128)(2,1)S(1)} %all-to-all-done.1.rows_ref.refs_0_, bf16[512,1024]{1,0:T(8,128)(2,1)} %bitcast.5.refs_0_, bf16[512,1024]{1,0:T(8,128)(2,1)} %collective-permute-done.refs_1_, ...), custom_call_target="tpu_custom_call" | custom-call | flops 3221225472 | bytes 12582912 | tf_op jit(solution)/shard_map/hidden_layer/pallas_call | solution.py:80
  85.6 8.4 %all-to-all-start.2 = ((bf16[8,256,256]{2,1,0:T(8,128)(2,1)}), bf16[8,256,256]{2,1,0:T(8,128)(2,1)}, u32[]{:S(2)}, u32[]{:S(2)}) async-start(bf16[8,256,256]{2,1,0:T(8,128)(2,1)} %copy-done.1), calls=%async_computation.2 | async-start | bytes 2097152 | tf_op jit(solution)/shard_map/all_to_all | solution.py:212
  94.0 2.2 %collective-permute-start.10 = (bf16[1,2,256,512]{3,2,1,0:T(8,128)(2,1)}, bf16[1,2,256,512]{3,2,1,0:T(8,128)(2,1)}, u32[]{:S(2)}, u32[]{:S(2)}) collective-permute-start(bf16[1,2,256,512]{3,2,1,0:T(8,128)(2,1)} %get-tuple-element.31), channel_id=1, source_target_pairs={{0,256},{256,0},{128,384},{384,128},{1,257},{257,1},{129,385},{385... | collective-permute-start | bytes 1572872 | tf_op jit(solution)/shard_map/ppermute | solution.py:208
  96.2 4.5 %collective-permute-start.7 = (bf16[2,256,1024]{2,1,0:T(8,128)(2,1)}, bf16[2,256,1024]{2,1,0:T(8,128)(2,1)}, u32[]{:S(2)}, u32[]{:S(2)}) collective-permute-start(bf16[2,256,1024]{2,1,0:T(8,128)(2,1)} %copy-done.2), channel_id=1, source_target_pairs={{0,128},{128,0},{256,384},{384,256},{1,129},{129,1},{257,385},{385... | collective-permute-start | bytes 3145736 | tf_op jit(solution)/shard_map/ppermute | solution.py:209
  100.6 3.1 %collective-permute-start.8 = (bf16[2,256,1024]{2,1,0:T(8,128)(2,1)}, bf16[2,256,1024]{2,1,0:T(8,128)(2,1)}, u32[]{:S(2)}, u32[]{:S(2)}) collective-permute-start(bf16[2,256,1024]{2,1,0:T(8,128)(2,1)} %copy-done.2), channel_id=1, source_target_pairs={{0,256},{256,0},{128,384},{384,128},{1,257},{257,1},{129,385},{385... | collective-permute-start | bytes 3145736 | tf_op jit(solution)/shard_map/ppermute | solution.py:210
  103.7 3.2 %all-to-all-done.2.terms_ref = bf16[8,256,256]{2,1,0:T(8,128)(2,1)} async-done(((bf16[8,256,256]{2,1,0:T(8,128)(2,1)}), bf16[8,256,256]{2,1,0:T(8,128)(2,1)}, u32[]{:S(2)}, u32[]{:S(2)}) %all-to-all-start.2) | async-done | bytes 1048608 | tf_op jit(solution)/shard_map/all_to_all | solution.py:212
  108.8 11.2 %all-to-all-start.3 = ((bf16[16,16,256]{2,1,0:T(8,128)(2,1)}), bf16[16,16,256]{2,1,0:T(8,128)(2,1)S(1)}, u32[]{:S(2)}, u32[]{:S(2)}) async-start(bf16[16,16,256]{2,1,0:T(8,128)(2,1)} %bitcast.17), calls=%async_computation.3 | async-start | bytes 262144 | tf_op jit(solution)/shard_map/all_to_all | solution.py:214
  120.0 9.6 %collective-permute-start.9 = (bf16[1,2,256,512]{3,2,1,0:T(8,128)(2,1)}, bf16[1,2,256,512]{3,2,1,0:T(8,128)(2,1)}, u32[]{:S(2)}, u32[]{:S(2)}) collective-permute-start(bf16[1,2,256,512]{3,2,1,0:T(8,128)(2,1)} %get-tuple-element.32), channel_id=1, source_target_pairs={{0,128},{128,0},{256,384},{384,256},{1,129},{129,1},{257,385},{385... | collective-permute-start | bytes 1572872 | tf_op jit(solution)/shard_map/ppermute | solution.py:206
  133.8 4.5 %collective-permute-done.8.refs_6_ = bf16[2,256,1024]{2,1,0:T(8,128)(2,1)} collective-permute-done((bf16[2,256,1024]{2,1,0:T(8,128)(2,1)}, bf16[2,256,1024]{2,1,0:T(8,128)(2,1)}, u32[]{:S(2)}, u32[]{:S(2)}) %collective-permute-start.8) | collective-permute-done | bytes 1048608 | tf_op jit(solution)/shard_map/ppermute | solution.py:210
  138.3 4.8 %collective-permute-start.12 = (bf16[2,256,1024]{2,1,0:T(8,128)(2,1)}, bf16[2,256,1024]{2,1,0:T(8,128)(2,1)}, u32[]{:S(2)}, u32[]{:S(2)}) collective-permute-start(bf16[2,256,1024]{2,1,0:T(8,128)(2,1)} %collective-permute-done.8.refs_6_), channel_id=1, source_target_pairs={{0,128},{128,0},{256,384},{384,256},{1,129},{129,1},{257,385},{385... | collective-permute-start | bytes 3145736 | tf_op jit(solution)/shard_map/ppermute | solution.py:221
  143.9 7.7 %all-to-all-start.4 = ((bf16[8,128,256]{2,1,0:T(8,128)(2,1)}), bf16[8,128,256]{2,1,0:T(8,128)(2,1)}, u32[]{:S(2)}, u32[]{:S(2)}) async-start(bf16[8,128,256]{2,1,0:T(8,128)(2,1)} %broadcast_in_dim.28), calls=%async_computation.4 | async-start | bytes 1048576 | tf_op jit(solution)/shard_map/all_to_all | solution.py:222
  152.8 5.5 %weight_grads.1 = (bf16[512,1024]{1,0:T(8,128)(2,1)}, bf16[1024,512]{1,0:T(8,128)(2,1)}) custom-call(bf16[4,2,256,512]{3,2,1,0:T(8,128)(2,1)S(1)} %all-to-all-done.1.rows_ref.refs_0_, bf16[1,2,256,512]{3,2,1,0:T(8,128)(2,1)} %collective-permute-done.9.refs_1_, bf16[1,2,256,512]{3,2,1,0:T(8,128)(2,1)S(1)} %collective-permute-done.6.refs_2_, ...), custom_call_target="tpu_custom_call" | custom-call | flops 2147483648 | bytes 8388608 | tf_op jit(solution)/shard_map/weight_grads/pallas_call | solution.py:139
  158.3 3.4 %all-to-all-done.4.pieces_ref = bf16[8,128,256]{2,1,0:T(8,128)(2,1)} async-done(((bf16[8,128,256]{2,1,0:T(8,128)(2,1)}), bf16[8,128,256]{2,1,0:T(8,128)(2,1)}, u32[]{:S(2)}, u32[]{:S(2)}) %all-to-all-start.4) | async-done | bytes 524320 | tf_op jit(solution)/shard_map/all_to_all | solution.py:222
  (34 shorter events, 18.0 us)
Async XLA Ops:
  0.6 1.1 copy-start
  4.0 38.6 %all-to-all-start = ((bf16[16,32,512]{2,1,0:T(8,128)(2,1)}), bf16[16,32,512]{2,1,0:T(8,128)(2,1)S(1)}, u32[]{:S(2)}, u32[]{:S(2)}) async-start(bf16[16,32,512]{2,1,0:T(8,128)(2,1)} %pad_maximum_fusion), calls=%async_computation | async-start | bytes 1048576 | tf_op jit(solution)/shard_map/all_to_all | solution.py:190
  19.7 39.9 %collective-permute-start.1 = (bf16[512,1024]{1,0:T(8,128)(2,1)}, bf16[512,1024]{1,0:T(8,128)(2,1)}, u32[]{:S(2)}, u32[]{:S(2)}) collective-permute-start(bf16[512,1024]{1,0:T(8,128)(2,1)} %bitcast.5.refs_0_), channel_id=1, source_target_pairs={{0,256},{256,0},{128,384},{384,128},{1,257},{257,1},{129,385},{385... | collective-permute-start | bytes 3145736 | tf_op jit(solution)/shard_map/ppermute | solution.py:196
  22.9 45.3 %collective-permute-start.4 = (bf16[1024,512]{1,0:T(8,128)(2,1)}, bf16[1024,512]{1,0:T(8,128)(2,1)}, u32[]{:S(2)}, u32[]{:S(2)}) collective-permute-start(bf16[1024,512]{1,0:T(8,128)(2,1)} %bitcast.6.refs_4_), channel_id=1, source_target_pairs={{0,256},{256,0},{128,384},{384,128},{1,257},{257,1},{129,385},{385... | collective-permute-start | bytes 3145736 | tf_op jit(solution)/shard_map/ppermute | solution.py:196
  44.1 27.8 %all-to-all-start.1 = ((bf16[4,2,256,512]{3,2,1,0:T(8,128)(2,1)}), bf16[4,2,256,512]{3,2,1,0:T(8,128)(2,1)S(1)}, u32[]{:S(2)}, u32[]{:S(2)}) async-start(bf16[4,2,256,512]{3,2,1,0:T(8,128)(2,1)} %broadcast_in_dim.27), calls=%async_computation.1 | async-start | bytes 4194304 | tf_op jit(solution)/shard_map/all_to_all | solution.py:193
  48.3 27.9 %collective-permute-start = (bf16[512,1024]{1,0:T(8,128)(2,1)}, bf16[512,1024]{1,0:T(8,128)(2,1)}, u32[]{:S(2)}, u32[]{:S(2)}) collective-permute-start(bf16[512,1024]{1,0:T(8,128)(2,1)} %bitcast.5.refs_0_), channel_id=1, source_target_pairs={{0,128},{128,0},{256,384},{384,256},{1,129},{129,1},{257,385},{385... | collective-permute-start | bytes 3145736 | tf_op jit(solution)/shard_map/ppermute | solution.py:197
  57.7 18.5 %collective-permute-start.3 = (bf16[1024,512]{1,0:T(8,128)(2,1)}, bf16[1024,512]{1,0:T(8,128)(2,1)}, u32[]{:S(2)}, u32[]{:S(2)}) collective-permute-start(bf16[1024,512]{1,0:T(8,128)(2,1)} %bitcast.6.refs_4_), channel_id=1, source_target_pairs={{0,128},{128,0},{256,384},{384,256},{1,129},{129,1},{257,385},{385... | collective-permute-start | bytes 3145736 | tf_op jit(solution)/shard_map/ppermute | solution.py:197
  59.7 16.6 %collective-permute-start.2 = (bf16[512,1024]{1,0:T(8,128)(2,1)}, bf16[512,1024]{1,0:T(8,128)(2,1)}, u32[]{:S(2)}, u32[]{:S(2)}) collective-permute-start(bf16[512,1024]{1,0:T(8,128)(2,1)} %collective-permute-done.1.refs_2_), channel_id=1, source_target_pairs={{0,128},{128,0},{256,384},{384,256},{1,129},{129,1},{257,385},{385... | collective-permute-start | bytes 3145736 | tf_op jit(solution)/shard_map/ppermute | solution.py:198
  68.1 8.1 %collective-permute-start.5 = (bf16[1024,512]{1,0:T(8,128)(2,1)}, bf16[1024,512]{1,0:T(8,128)(2,1)}, u32[]{:S(2)}, u32[]{:S(2)}) collective-permute-start(bf16[1024,512]{1,0:T(8,128)(2,1)} %collective-permute-done.4.refs_6_), channel_id=1, source_target_pairs={{0,128},{128,0},{256,384},{384,256},{1,129},{129,1},{257,385},{385... | collective-permute-start | bytes 3145736 | tf_op jit(solution)/shard_map/ppermute | solution.py:198
  73.1 12.5 %collective-permute-start.6 = (bf16[1,2,256,512]{3,2,1,0:T(8,128)(2,1)S(1)}, bf16[1,2,256,512]{3,2,1,0:T(8,128)(2,1)S(1)}, u32[]{:S(2)}, u32[]{:S(2)}) collective-permute-start(bf16[1,2,256,512]{3,2,1,0:T(8,128)(2,1)S(1)} %get-tuple-element.33), channel_id=1, source_target_pairs={{0,256},{256,0},{128,384},{384,128},{1,257},{257,1},{129,385},{385... | collective-permute-start | bytes 1572872 | tf_op jit(solution)/shard_map/ppermute | solution.py:207
  83.6 1.0 copy-start.1
  84.6 1.0 copy-start.2
  85.6 21.3 %all-to-all-start.2 = ((bf16[8,256,256]{2,1,0:T(8,128)(2,1)}), bf16[8,256,256]{2,1,0:T(8,128)(2,1)}, u32[]{:S(2)}, u32[]{:S(2)}) async-start(bf16[8,256,256]{2,1,0:T(8,128)(2,1)} %copy-done.1), calls=%async_computation.2 | async-start | bytes 2097152 | tf_op jit(solution)/shard_map/all_to_all | solution.py:212
  94.0 35.7 %collective-permute-start.10 = (bf16[1,2,256,512]{3,2,1,0:T(8,128)(2,1)}, bf16[1,2,256,512]{3,2,1,0:T(8,128)(2,1)}, u32[]{:S(2)}, u32[]{:S(2)}) collective-permute-start(bf16[1,2,256,512]{3,2,1,0:T(8,128)(2,1)} %get-tuple-element.31), channel_id=1, source_target_pairs={{0,256},{256,0},{128,384},{384,128},{1,257},{257,1},{129,385},{385... | collective-permute-start | bytes 1572872 | tf_op jit(solution)/shard_map/ppermute | solution.py:208
  96.2 37.6 %collective-permute-start.7 = (bf16[2,256,1024]{2,1,0:T(8,128)(2,1)}, bf16[2,256,1024]{2,1,0:T(8,128)(2,1)}, u32[]{:S(2)}, u32[]{:S(2)}) collective-permute-start(bf16[2,256,1024]{2,1,0:T(8,128)(2,1)} %copy-done.2), channel_id=1, source_target_pairs={{0,128},{128,0},{256,384},{384,256},{1,129},{129,1},{257,385},{385... | collective-permute-start | bytes 3145736 | tf_op jit(solution)/shard_map/ppermute | solution.py:209
  100.6 37.6 %collective-permute-start.8 = (bf16[2,256,1024]{2,1,0:T(8,128)(2,1)}, bf16[2,256,1024]{2,1,0:T(8,128)(2,1)}, u32[]{:S(2)}, u32[]{:S(2)}) collective-permute-start(bf16[2,256,1024]{2,1,0:T(8,128)(2,1)} %copy-done.2), channel_id=1, source_target_pairs={{0,256},{256,0},{128,384},{384,128},{1,257},{257,1},{129,385},{385... | collective-permute-start | bytes 3145736 | tf_op jit(solution)/shard_map/ppermute | solution.py:210
  108.8 23.1 %all-to-all-start.3 = ((bf16[16,16,256]{2,1,0:T(8,128)(2,1)}), bf16[16,16,256]{2,1,0:T(8,128)(2,1)S(1)}, u32[]{:S(2)}, u32[]{:S(2)}) async-start(bf16[16,16,256]{2,1,0:T(8,128)(2,1)} %bitcast.17), calls=%async_computation.3 | async-start | bytes 262144 | tf_op jit(solution)/shard_map/all_to_all | solution.py:214
  120.0 12.2 %collective-permute-start.9 = (bf16[1,2,256,512]{3,2,1,0:T(8,128)(2,1)}, bf16[1,2,256,512]{3,2,1,0:T(8,128)(2,1)}, u32[]{:S(2)}, u32[]{:S(2)}) collective-permute-start(bf16[1,2,256,512]{3,2,1,0:T(8,128)(2,1)} %get-tuple-element.32), channel_id=1, source_target_pairs={{0,128},{128,0},{256,384},{384,256},{1,129},{129,1},{257,385},{385... | collective-permute-start | bytes 1572872 | tf_op jit(solution)/shard_map/ppermute | solution.py:206
  129.6 4.1 %collective-permute-start.11 = (bf16[1,2,256,512]{3,2,1,0:T(8,128)(2,1)}, bf16[1,2,256,512]{3,2,1,0:T(8,128)(2,1)}, u32[]{:S(2)}, u32[]{:S(2)}) collective-permute-start(bf16[1,2,256,512]{3,2,1,0:T(8,128)(2,1)} %collective-permute-done.10), channel_id=1, source_target_pairs={{0,128},{128,0},{256,384},{384,256},{1,129},{129,1},{257,385},{385... | collective-permute-start | bytes 1572872 | tf_op jit(solution)/shard_map/ppermute | solution.py:208
  138.3 13.3 %collective-permute-start.12 = (bf16[2,256,1024]{2,1,0:T(8,128)(2,1)}, bf16[2,256,1024]{2,1,0:T(8,128)(2,1)}, u32[]{:S(2)}, u32[]{:S(2)}) collective-permute-start(bf16[2,256,1024]{2,1,0:T(8,128)(2,1)} %collective-permute-done.8.refs_6_), channel_id=1, source_target_pairs={{0,128},{128,0},{256,384},{384,256},{1,129},{129,1},{257,385},{385... | collective-permute-start | bytes 3145736 | tf_op jit(solution)/shard_map/ppermute | solution.py:221
  143.9 17.8 %all-to-all-start.4 = ((bf16[8,128,256]{2,1,0:T(8,128)(2,1)}), bf16[8,128,256]{2,1,0:T(8,128)(2,1)}, u32[]{:S(2)}, u32[]{:S(2)}) async-start(bf16[8,128,256]{2,1,0:T(8,128)(2,1)} %broadcast_in_dim.28), calls=%async_computation.4 | async-start | bytes 1048576 | tf_op jit(solution)/shard_map/all_to_all | solution.py:222
  151.6 1.2 copy-start.3

commit v4 on v3

--- a/solution.py
+++ b/solution.py
@@ -17,10 +17,10 @@
     return (preact * normal_cdf, normal_cdf + preact * density)
 
 
-def route_table(routes, slots, experts_count, capacity):
+def route_table(routes, slots, rows, capacity):
     position = jnp.where(slots < capacity, routes * capacity + slots, -1)
-    targets = lax.broadcasted_iota(jnp.int32, (experts_count * capacity, routes.shape[0]), 0)
-    return (targets == position[None, :]).astype(jnp.bfloat16)
+    targets = lax.broadcasted_iota(jnp.int32, (rows, routes.shape[1]), 0)
+    return jnp.where(targets == position, 1.0, 0.0).astype(jnp.bfloat16)
 
 
 def dot(left, right, left_dim, right_dim):
@@ -30,6 +30,38 @@
         (((left_dim,), (right_dim,)), ((), ())),
         preferred_element_type=jnp.float32,
     )
+
+
+def dispatch_kernel(column_ref, routes_ref, slots_ref, gate_ref, tokens_ref, grads_ref, out_ref):
+    experts, both, depth = out_ref.shape
+    capacity = both // 2
+    group = tokens_ref.shape[0]
+    table = route_table(routes_ref[...], slots_ref[...], experts * capacity, capacity)
+    across = lax.broadcasted_iota(jnp.int32, (group, group), 1)
+    down = lax.broadcasted_iota(jnp.int32, (group, group), 0)
+    gate = jnp.sum(jnp.where(across == down, gate_ref[...], 0.0), axis=1, keepdims=True)
+    scaled = (grads_ref[...].astype(jnp.float32) * gate).astype(jnp.bfloat16)
+    for place, values in ((0, tokens_ref[...]), (capacity, scaled)):
+        sent = dot(table, values, 1, 0).astype(jnp.bfloat16)
+        out_ref[:, pl.ds(place, capacity), :] = sent.reshape(experts, capacity, depth)
+
+
+def dispatch(column, routes, slots, gate, tokens, cotangent, experts, capacity, depth):
+    group = tokens.shape[0]
+    row = pl.BlockSpec((1, group), lambda j, _: (0, 0))
+    block = pl.BlockSpec((group, depth), lambda j, column: (0, column[0]))
+    spec = pltpu.PrefetchScalarGridSpec(
+        num_scalar_prefetch=1,
+        grid=(1,),
+        in_specs=[row] * 3 + [block] * 2,
+        out_specs=pl.BlockSpec((experts, 2 * capacity, depth), lambda j, _: (0, 0, 0)),
+    )
+    return pl.pallas_call(
+        dispatch_kernel,
+        grid_spec=spec,
+        out_shape=jax.ShapeDtypeStruct((experts, 2 * capacity, depth), jnp.bfloat16),
+        name="dispatch",
+    )(column, routes, slots, gate, tokens, cotangent)
 
 
 def hidden_kernel(place_ref, rows_ref, *refs):
@@ -173,20 +205,9 @@
     y = lax.axis_index("tensor").astype(jnp.int32) % ring
     rings = [[i * ring + j for j in range(ring)] for i in range(halves)]
 
-    start = (replica ^ y) * depth
-    own_tokens = lax.dynamic_slice_in_dim(tokens, start, depth, 1)
-    own_cotangent = lax.dynamic_slice_in_dim(cotangent, start, depth, 1)
-    scaled = (own_cotangent.astype(jnp.float32) * gate[:, None]).astype(jnp.bfloat16)
-    table = route_table(routes, slots, experts, capacity)
-    sent_tokens = dot(table, own_tokens, 1, 0).astype(jnp.bfloat16)
-    sent_grads = dot(table, scaled, 1, 0).astype(jnp.bfloat16)
-    sent = jnp.concatenate(
-        [
-            sent_tokens.reshape(experts, capacity, depth),
-            sent_grads.reshape(experts, capacity, depth),
-        ],
-        axis=1,
-    )
+    routes, slots, gate = (value.reshape(1, group) for value in (routes, slots, gate))
+    column = (replica ^ y).reshape(1)
+    sent = dispatch(column, routes, slots, gate, tokens, cotangent, experts, capacity, depth)
     came = lax.all_to_all(sent, "expert", 0, 0, tiled=True)
     came = came.reshape(experts, 2, capacity, depth).transpose(1, 0, 2, 3)
     copies = jnp.broadcast_to(came.reshape(1, 2, count, depth), (ring, 2, count, depth))
@@ -214,6 +235,7 @@
     returned = lax.all_to_all(
         row_grads.reshape(experts, capacity, block), "expert", 0, 0, tiled=True
     ).reshape(count, block)
+    table = route_table(routes, slots, count, capacity)
     own_grads = dot(table, returned, 0, 0).astype(jnp.bfloat16)
     own_grads, acts1, acts2, rows1, rows3 = lax.optimization_barrier(
         (own_grads, acts1, acts2, rows1, rows3)

time: 165 us -> 164 us (level)
  Pallas kernels: 16.7 us -> 19.6 us
  starting transfers between devices: 99.1 us -> 101 us
    pallas_call x0 -> x1, Pallas kernels: none -> 2.21 us  [dispatch(): pl.pallas_call(dispatch_kernel, grid_spec=spec, out_shape=jax.ShapeDtypeS...]
    unnamed x8 -> x14, local copies, waits for them, and re-layouts: 3.48 us -> 2.83 us
where the time goes in v4:
time: 164 us; the launch traced here: 163 us
  starting transfers between devices  101 us (62%)
  waiting for transfers between devices  35.2 us (21%)
  Pallas kernels  19.6 us (12%)
  local copies, waits for them, and re-layouts  6.39 us (4%)
    all_to_all x1, waiting for transfers between devices, shards(): came = lax.all_to_all(sent, 'expert', 0, 0, tiled=True)  17.5 us
    all_to_all x1, starting transfers between devices, shards(): came = lax.all_to_all(sent, 'expert', 0, 0, tiled=True)  15.7 us
    all_to_all x1, starting transfers between devices, shards(): lax.all_to_all(row_grads.reshape(experts, capacity, block), 'expert', 0,...  12.1 us
    ppermute x1, starting transfers between devices, shards(): rows1 = lax.ppermute(rows[1:2], 'dp', BESIDE)  9.62 us
    ppermute x1, starting transfers between devices, shards(): lax.ppermute(first0, 'dp', BESIDE)  9.4 us
    all_to_all x1, starting transfers between devices, shards(): terms = lax.all_to_all(partial_rows, 'tensor', 0, 0, tiled=True)  8.57 us
    pallas_call x1, Pallas kernels, hidden_layer(): pl.pallas_call(hidden_kernel, grid_spec=spec, out_shape=[jax.ShapeDtypeSt...  8.07 us
    all_to_all x1, starting transfers between devices, shards(): lax.all_to_all(jnp.broadcast_to(own_grads[None], (parts, group, block)),...  7.26 us
  transfers between devices with their start and end apart: 18, of which 7 were waited for; matrix products, arithmetic and copies ran while one was open for 2% of the time, Pallas kernels for 9%

profile of v4, /device:TPU:1, one launch (start us, length us, event | category | flops | bytes accessed | tf_op | source)
XLA Modules:
  0.0 163.0 jit_solution(8963794439359677879)
XLA Ops:
  0.7 2.2 %dispatch.1 = bf16[16,32,512]{2,1,0:T(8,128)(2,1)} custom-call(s32[1]{0:T(128)} %bitcast.column_ref, s32[1,128]{1,0:T(1,128)} %bitcast.23, s32[1,128]{1,0:T(1,128)} %bitcast.24, f32[1,128]{1,0:T(1,128)} %bitcast.22, bf16[128,2048]{1,0:T(8,128)(2,1)} %tokens_ref.1, bf16[128,2048]{1,0:T(8,128)(2,1)} %grads_ref.1), custom_call_target="tpu_custom_call" | custom-call | tf_op jit(solution)/shard_map/dispatch/pallas_call | solution.py:59
  2.9 15.7 %all-to-all-start = ((bf16[16,32,512]{2,1,0:T(8,128)(2,1)}), bf16[16,32,512]{2,1,0:T(8,128)(2,1)S(1)}, u32[]{:S(2)}, u32[]{:S(2)}) async-start(bf16[16,32,512]{2,1,0:T(8,128)(2,1)} %dispatch.1), calls=%async_computation | async-start | bytes 1048576 | tf_op jit(solution)/shard_map/all_to_all | solution.py:211
  18.6 3.1 %collective-permute-start.1 = (bf16[512,1024]{1,0:T(8,128)(2,1)S(1)}, bf16[512,1024]{1,0:T(8,128)(2,1)}, u32[]{:S(2)}, u32[]{:S(2)}) collective-permute-start(bf16[512,1024]{1,0:T(8,128)(2,1)S(1)} %bitcast.15), channel_id=1, source_target_pairs={{0,256},{256,0},{128,384},{384,128},{1,257},{257,1},{129,385},{385... | collective-permute-start | bytes 3145736 | tf_op jit(solution)/shard_map/ppermute | solution.py:217
  21.8 2.2 %collective-permute-start.4 = (bf16[1024,512]{1,0:T(8,128)(2,1)}, bf16[1024,512]{1,0:T(8,128)(2,1)}, u32[]{:S(2)}, u32[]{:S(2)}) collective-permute-start(bf16[1024,512]{1,0:T(8,128)(2,1)} %bitcast.8.refs_4_), channel_id=1, source_target_pairs={{0,256},{256,0},{128,384},{384,128},{1,257},{257,1},{129,385},{385... | collective-permute-start | bytes 3145736 | tf_op jit(solution)/shard_map/ppermute | solution.py:217
  23.9 17.5 %all-to-all-done = bf16[16,32,512]{2,1,0:T(8,128)(2,1)S(1)} async-done(((bf16[16,32,512]{2,1,0:T(8,128)(2,1)}), bf16[16,32,512]{2,1,0:T(8,128)(2,1)S(1)}, u32[]{:S(2)}, u32[]{:S(2)}) %all-to-all-start) | async-done | bytes 524320 | tf_op jit(solution)/shard_map/all_to_all | solution.py:211
  43.0 4.2 %all-to-all-start.1 = ((bf16[4,2,256,512]{3,2,1,0:T(8,128)(2,1)}), bf16[4,2,256,512]{3,2,1,0:T(8,128)(2,1)S(1)}, u32[]{:S(2)}, u32[]{:S(2)}) async-start(bf16[4,2,256,512]{3,2,1,0:T(8,128)(2,1)} %broadcast_in_dim.35), calls=%async_computation.1 | async-start | bytes 4194304 | tf_op jit(solution)/shard_map/all_to_all | solution.py:214
  47.2 9.4 %collective-permute-start = (bf16[512,1024]{1,0:T(8,128)(2,1)S(1)}, bf16[512,1024]{1,0:T(8,128)(2,1)}, u32[]{:S(2)}, u32[]{:S(2)}) collective-permute-start(bf16[512,1024]{1,0:T(8,128)(2,1)S(1)} %bitcast.16), channel_id=1, source_target_pairs={{0,128},{128,0},{256,384},{384,256},{1,129},{129,1},{257,385},{385... | collective-permute-start | bytes 3145736 | tf_op jit(solution)/shard_map/ppermute | solution.py:218
  58.6 2.4 %collective-permute-start.2 = (bf16[512,1024]{1,0:T(8,128)(2,1)}, bf16[512,1024]{1,0:T(8,128)(2,1)}, u32[]{:S(2)}, u32[]{:S(2)}) collective-permute-start(bf16[512,1024]{1,0:T(8,128)(2,1)} %collective-permute-done.1.refs_2_), channel_id=1, source_target_pairs={{0,128},{128,0},{256,384},{384,256},{1,129},{129,1},{257,385},{385... | collective-permute-start | bytes 3145736 | tf_op jit(solution)/shard_map/ppermute | solution.py:219
  61.0 5.8 %collective-permute-done.4.refs_6_ = bf16[1024,512]{1,0:T(8,128)(2,1)} collective-permute-done((bf16[1024,512]{1,0:T(8,128)(2,1)}, bf16[1024,512]{1,0:T(8,128)(2,1)}, u32[]{:S(2)}, u32[]{:S(2)}) %collective-permute-start.4) | collective-permute-done | bytes 1048608 | tf_op jit(solution)/shard_map/ppermute | solution.py:217
  66.8 3.8 %collective-permute-start.5 = (bf16[1024,512]{1,0:T(8,128)(2,1)}, bf16[1024,512]{1,0:T(8,128)(2,1)}, u32[]{:S(2)}, u32[]{:S(2)}) collective-permute-start(bf16[1024,512]{1,0:T(8,128)(2,1)} %collective-permute-done.4.refs_6_), channel_id=1, source_target_pairs={{0,128},{128,0},{256,384},{384,256},{1,129},{129,1},{257,385},{385... | collective-permute-start | bytes 3145736 | tf_op jit(solution)/shard_map/ppermute | solution.py:219
  71.7 3.1 %collective-permute-start.6 = (bf16[1,2,256,512]{3,2,1,0:T(8,128)(2,1)S(1)}, bf16[1,2,256,512]{3,2,1,0:T(8,128)(2,1)S(1)}, u32[]{:S(2)}, u32[]{:S(2)}) collective-permute-start(bf16[1,2,256,512]{3,2,1,0:T(8,128)(2,1)S(1)} %get-tuple-element.33), channel_id=1, source_target_pairs={{0,256},{256,0},{128,384},{384,128},{1,257},{257,1},{129,385},{385... | collective-permute-start | bytes 1572872 | tf_op jit(solution)/shard_map/ppermute | solution.py:228
  74.9 8.1 %hidden_layer.1 = (bf16[2,256,1024]{2,1,0:T(8,128)(2,1)S(1)}, bf16[8,256,256]{2,1,0:T(8,128)(2,1)}) custom-call(s32[8]{0:T(128)S(1)} %fusion.3.place_ref, bf16[4,2,256,512]{3,2,1,0:T(8,128)(2,1)S(1)} %all-to-all-done.1.rows_ref.refs_0_, bf16[512,1024]{1,0:T(8,128)(2,1)S(1)} %bitcast.17, bf16[512,1024]{1,0:T(8,128)(2,1)} %collective-permute-done.refs_1_, ...), custom_call_target="tpu_custom_call" | custom-call | flops 3221225472 | bytes 12582912 | tf_op jit(solution)/shard_map/hidden_layer/pallas_call | solution.py:112
  84.8 8.6 %all-to-all-start.2 = ((bf16[8,256,256]{2,1,0:T(8,128)(2,1)}), bf16[8,256,256]{2,1,0:T(8,128)(2,1)}, u32[]{:S(2)}, u32[]{:S(2)}) async-start(bf16[8,256,256]{2,1,0:T(8,128)(2,1)} %get-tuple-element.18), calls=%async_computation.2 | async-start | bytes 2097152 | tf_op jit(solution)/shard_map/all_to_all | solution.py:233
  93.3 2.2 %collective-permute-start.10 = (bf16[1,2,256,512]{3,2,1,0:T(8,128)(2,1)}, bf16[1,2,256,512]{3,2,1,0:T(8,128)(2,1)}, u32[]{:S(2)}, u32[]{:S(2)}) collective-permute-start(bf16[1,2,256,512]{3,2,1,0:T(8,128)(2,1)} %get-tuple-element.31), channel_id=1, source_target_pairs={{0,256},{256,0},{128,384},{384,128},{1,257},{257,1},{129,385},{385... | collective-permute-start | bytes 1572872 | tf_op jit(solution)/shard_map/ppermute | solution.py:229
  95.6 4.7 %collective-permute-start.7 = (bf16[2,256,1024]{2,1,0:T(8,128)(2,1)S(1)}, bf16[2,256,1024]{2,1,0:T(8,128)(2,1)}, u32[]{:S(2)}, u32[]{:S(2)}) collective-permute-start(bf16[2,256,1024]{2,1,0:T(8,128)(2,1)S(1)} %copy-done.2), channel_id=1, source_target_pairs={{0,128},{128,0},{256,384},{384,256},{1,129},{129,1},{257,385},{385... | collective-permute-start | bytes 3145736 | tf_op jit(solution)/shard_map/ppermute | solution.py:230
  100.3 3.1 %collective-permute-start.8 = (bf16[2,256,1024]{2,1,0:T(8,128)(2,1)S(1)}, bf16[2,256,1024]{2,1,0:T(8,128)(2,1)}, u32[]{:S(2)}, u32[]{:S(2)}) collective-permute-start(bf16[2,256,1024]{2,1,0:T(8,128)(2,1)S(1)} %copy-done.2), channel_id=1, source_target_pairs={{0,256},{256,0},{128,384},{384,128},{1,257},{257,1},{129,385},{385... | collective-permute-start | bytes 3145736 | tf_op jit(solution)/shard_map/ppermute | solution.py:231
  103.3 2.5 %all-to-all-done.2.terms_ref = bf16[8,256,256]{2,1,0:T(8,128)(2,1)} async-done(((bf16[8,256,256]{2,1,0:T(8,128)(2,1)}), bf16[8,256,256]{2,1,0:T(8,128)(2,1)}, u32[]{:S(2)}, u32[]{:S(2)}) %all-to-all-start.2) | async-done | bytes 1048608 | tf_op jit(solution)/shard_map/all_to_all | solution.py:233
  107.7 12.1 %all-to-all-start.3 = ((bf16[16,16,256]{2,1,0:T(8,128)(2,1)}), bf16[16,16,256]{2,1,0:T(8,128)(2,1)S(1)}, u32[]{:S(2)}, u32[]{:S(2)}) async-start(bf16[16,16,256]{2,1,0:T(8,128)(2,1)} %bitcast.20), calls=%async_computation.3 | async-start | bytes 262144 | tf_op jit(solution)/shard_map/all_to_all | solution.py:235
  119.8 9.6 %collective-permute-start.9 = (bf16[1,2,256,512]{3,2,1,0:T(8,128)(2,1)}, bf16[1,2,256,512]{3,2,1,0:T(8,128)(2,1)}, u32[]{:S(2)}, u32[]{:S(2)}) collective-permute-start(bf16[1,2,256,512]{3,2,1,0:T(8,128)(2,1)} %get-tuple-element.32), channel_id=1, source_target_pairs={{0,128},{128,0},{256,384},{384,256},{1,129},{129,1},{257,385},{385... | collective-permute-start | bytes 1572872 | tf_op jit(solution)/shard_map/ppermute | solution.py:227
  133.6 3.8 %collective-permute-done.8.refs_6_ = bf16[2,256,1024]{2,1,0:T(8,128)(2,1)} collective-permute-done((bf16[2,256,1024]{2,1,0:T(8,128)(2,1)S(1)}, bf16[2,256,1024]{2,1,0:T(8,128)(2,1)}, u32[]{:S(2)}, u32[]{:S(2)}) %collective-permute-start.8) | collective-permute-done | bytes 1048608 | tf_op jit(solution)/shard_map/ppermute | solution.py:231
  137.4 5.4 %collective-permute-start.12 = (bf16[2,256,1024]{2,1,0:T(8,128)(2,1)}, bf16[2,256,1024]{2,1,0:T(8,128)(2,1)}, u32[]{:S(2)}, u32[]{:S(2)}) collective-permute-start(bf16[2,256,1024]{2,1,0:T(8,128)(2,1)} %collective-permute-done.8.refs_6_), channel_id=1, source_target_pairs={{0,128},{128,0},{256,384},{384,256},{1,129},{129,1},{257,385},{385... | collective-permute-start | bytes 3145736 | tf_op jit(solution)/shard_map/ppermute | solution.py:243
  143.7 7.3 %all-to-all-start.4 = ((bf16[8,128,256]{2,1,0:T(8,128)(2,1)}), bf16[8,128,256]{2,1,0:T(8,128)(2,1)}, u32[]{:S(2)}, u32[]{:S(2)}) async-start(bf16[8,128,256]{2,1,0:T(8,128)(2,1)} %broadcast_in_dim.36), calls=%async_computation.4 | async-start | bytes 1048576 | tf_op jit(solution)/shard_map/all_to_all | solution.py:244
  152.0 5.5 %weight_grads.1 = (bf16[512,1024]{1,0:T(8,128)(2,1)}, bf16[1024,512]{1,0:T(8,128)(2,1)}) custom-call(bf16[4,2,256,512]{3,2,1,0:T(8,128)(2,1)S(1)} %all-to-all-done.1.rows_ref.refs_0_, bf16[1,2,256,512]{3,2,1,0:T(8,128)(2,1)} %collective-permute-done.9.refs_1_, bf16[1,2,256,512]{3,2,1,0:T(8,128)(2,1)S(1)} %copy-done.4, ...), custom_call_target="tpu_custom_call" | custom-call | flops 2147483648 | bytes 8388608 | tf_op jit(solution)/shard_map/weight_grads/pallas_call | solution.py:171
  157.5 3.6 %all-to-all-done.4.pieces_ref = bf16[8,128,256]{2,1,0:T(8,128)(2,1)} async-done(((bf16[8,128,256]{2,1,0:T(8,128)(2,1)}), bf16[8,128,256]{2,1,0:T(8,128)(2,1)}, u32[]{:S(2)}, u32[]{:S(2)}) %all-to-all-start.4) | async-done | bytes 524320 | tf_op jit(solution)/shard_map/all_to_all | solution.py:244
  (38 shorter events, 16.2 us)
Async XLA Ops:
  0.6 18.0 %copy-start = (bf16[1,512,1024]{2,1,0:T(8,128)(2,1)S(1)}, bf16[1,512,1024]{2,1,0:T(8,128)(2,1)}, u32[]{:S(2)}) copy-start(bf16[1,512,1024]{2,1,0:T(8,128)(2,1)} %param.12) | copy-start | bytes 3145732
  2.9 38.6 %all-to-all-start = ((bf16[16,32,512]{2,1,0:T(8,128)(2,1)}), bf16[16,32,512]{2,1,0:T(8,128)(2,1)S(1)}, u32[]{:S(2)}, u32[]{:S(2)}) async-start(bf16[16,32,512]{2,1,0:T(8,128)(2,1)} %dispatch.1), calls=%async_computation | async-start | bytes 1048576 | tf_op jit(solution)/shard_map/all_to_all | solution.py:211
  18.6 39.9 %collective-permute-start.1 = (bf16[512,1024]{1,0:T(8,128)(2,1)S(1)}, bf16[512,1024]{1,0:T(8,128)(2,1)}, u32[]{:S(2)}, u32[]{:S(2)}) collective-permute-start(bf16[512,1024]{1,0:T(8,128)(2,1)S(1)} %bitcast.15), channel_id=1, source_target_pairs={{0,256},{256,0},{128,384},{384,128},{1,257},{257,1},{129,385},{385... | collective-permute-start | bytes 3145736 | tf_op jit(solution)/shard_map/ppermute | solution.py:217
  21.8 45.1 %collective-permute-start.4 = (bf16[1024,512]{1,0:T(8,128)(2,1)}, bf16[1024,512]{1,0:T(8,128)(2,1)}, u32[]{:S(2)}, u32[]{:S(2)}) collective-permute-start(bf16[1024,512]{1,0:T(8,128)(2,1)} %bitcast.8.refs_4_), channel_id=1, source_target_pairs={{0,256},{256,0},{128,384},{384,128},{1,257},{257,1},{129,385},{385... | collective-permute-start | bytes 3145736 | tf_op jit(solution)/shard_map/ppermute | solution.py:217
  43.0 27.6 %all-to-all-start.1 = ((bf16[4,2,256,512]{3,2,1,0:T(8,128)(2,1)}), bf16[4,2,256,512]{3,2,1,0:T(8,128)(2,1)S(1)}, u32[]{:S(2)}, u32[]{:S(2)}) async-start(bf16[4,2,256,512]{3,2,1,0:T(8,128)(2,1)} %broadcast_in_dim.35), calls=%async_computation.1 | async-start | bytes 4194304 | tf_op jit(solution)/shard_map/all_to_all | solution.py:214
  47.2 27.7 %collective-permute-start = (bf16[512,1024]{1,0:T(8,128)(2,1)S(1)}, bf16[512,1024]{1,0:T(8,128)(2,1)}, u32[]{:S(2)}, u32[]{:S(2)}) collective-permute-start(bf16[512,1024]{1,0:T(8,128)(2,1)S(1)} %bitcast.16), channel_id=1, source_target_pairs={{0,128},{128,0},{256,384},{384,256},{1,129},{129,1},{257,385},{385... | collective-permute-start | bytes 3145736 | tf_op jit(solution)/shard_map/ppermute | solution.py:218
  56.6 18.3 %collective-permute-start.3 = (bf16[1024,512]{1,0:T(8,128)(2,1)}, bf16[1024,512]{1,0:T(8,128)(2,1)}, u32[]{:S(2)}, u32[]{:S(2)}) collective-permute-start(bf16[1024,512]{1,0:T(8,128)(2,1)} %bitcast.8.refs_4_), channel_id=1, source_target_pairs={{0,128},{128,0},{256,384},{384,256},{1,129},{129,1},{257,385},{385... | collective-permute-start | bytes 3145736 | tf_op jit(solution)/shard_map/ppermute | solution.py:218
  58.6 16.3 %collective-permute-start.2 = (bf16[512,1024]{1,0:T(8,128)(2,1)}, bf16[512,1024]{1,0:T(8,128)(2,1)}, u32[]{:S(2)}, u32[]{:S(2)}) collective-permute-start(bf16[512,1024]{1,0:T(8,128)(2,1)} %collective-permute-done.1.refs_2_), channel_id=1, source_target_pairs={{0,128},{128,0},{256,384},{384,256},{1,129},{129,1},{257,385},{385... | collective-permute-start | bytes 3145736 | tf_op jit(solution)/shard_map/ppermute | solution.py:219
  66.8 8.1 %collective-permute-start.5 = (bf16[1024,512]{1,0:T(8,128)(2,1)}, bf16[1024,512]{1,0:T(8,128)(2,1)}, u32[]{:S(2)}, u32[]{:S(2)}) collective-permute-start(bf16[1024,512]{1,0:T(8,128)(2,1)} %collective-permute-done.4.refs_6_), channel_id=1, source_target_pairs={{0,128},{128,0},{256,384},{384,256},{1,129},{129,1},{257,385},{385... | collective-permute-start | bytes 3145736 | tf_op jit(solution)/shard_map/ppermute | solution.py:219
  71.7 12.2 %collective-permute-start.6 = (bf16[1,2,256,512]{3,2,1,0:T(8,128)(2,1)S(1)}, bf16[1,2,256,512]{3,2,1,0:T(8,128)(2,1)S(1)}, u32[]{:S(2)}, u32[]{:S(2)}) collective-permute-start(bf16[1,2,256,512]{3,2,1,0:T(8,128)(2,1)S(1)} %get-tuple-element.33), channel_id=1, source_target_pairs={{0,256},{256,0},{128,384},{384,128},{1,257},{257,1},{129,385},{385... | collective-permute-start | bytes 1572872 | tf_op jit(solution)/shard_map/ppermute | solution.py:228
  83.0 1.0 copy-start.1
  84.0 47.5 %copy-start.5 = (s32[128]{0:T(128)S(1)}, s32[128]{0:T(128)}, u32[]{:S(2)}) copy-start(s32[128]{0:T(128)} %param.8) | copy-start | bytes 1540
  84.0 47.5 %copy-start.6 = (s32[128]{0:T(128)S(1)}, s32[128]{0:T(128)}, u32[]{:S(2)}) copy-start(s32[128]{0:T(128)} %param.9) | copy-start | bytes 1540
  84.8 10.8 %copy-start.2 = (bf16[2,256,1024]{2,1,0:T(8,128)(2,1)S(1)}, bf16[2,256,1024]{2,1,0:T(8,128)(2,1)}, u32[]{:S(2)}) copy-start(bf16[2,256,1024]{2,1,0:T(8,128)(2,1)} %copy-done.1) | copy-start | bytes 3145732
  84.8 21.0 %all-to-all-start.2 = ((bf16[8,256,256]{2,1,0:T(8,128)(2,1)}), bf16[8,256,256]{2,1,0:T(8,128)(2,1)}, u32[]{:S(2)}, u32[]{:S(2)}) async-start(bf16[8,256,256]{2,1,0:T(8,128)(2,1)} %get-tuple-element.18), calls=%async_computation.2 | async-start | bytes 2097152 | tf_op jit(solution)/shard_map/all_to_all | solution.py:233
  93.3 36.1 %collective-permute-start.10 = (bf16[1,2,256,512]{3,2,1,0:T(8,128)(2,1)}, bf16[1,2,256,512]{3,2,1,0:T(8,128)(2,1)}, u32[]{:S(2)}, u32[]{:S(2)}) collective-permute-start(bf16[1,2,256,512]{3,2,1,0:T(8,128)(2,1)} %get-tuple-element.31), channel_id=1, source_target_pairs={{0,256},{256,0},{128,384},{384,128},{1,257},{257,1},{129,385},{385... | collective-permute-start | bytes 1572872 | tf_op jit(solution)/shard_map/ppermute | solution.py:229
  95.6 38.1 %collective-permute-start.7 = (bf16[2,256,1024]{2,1,0:T(8,128)(2,1)S(1)}, bf16[2,256,1024]{2,1,0:T(8,128)(2,1)}, u32[]{:S(2)}, u32[]{:S(2)}) collective-permute-start(bf16[2,256,1024]{2,1,0:T(8,128)(2,1)S(1)} %copy-done.2), channel_id=1, source_target_pairs={{0,128},{128,0},{256,384},{384,256},{1,129},{129,1},{257,385},{385... | collective-permute-start | bytes 3145736 | tf_op jit(solution)/shard_map/ppermute | solution.py:230
  100.3 37.1 %collective-permute-start.8 = (bf16[2,256,1024]{2,1,0:T(8,128)(2,1)S(1)}, bf16[2,256,1024]{2,1,0:T(8,128)(2,1)}, u32[]{:S(2)}, u32[]{:S(2)}) collective-permute-start(bf16[2,256,1024]{2,1,0:T(8,128)(2,1)S(1)} %copy-done.2), channel_id=1, source_target_pairs={{0,256},{256,0},{128,384},{384,128},{1,257},{257,1},{129,385},{385... | collective-permute-start | bytes 3145736 | tf_op jit(solution)/shard_map/ppermute | solution.py:231
  107.7 24.1 %all-to-all-start.3 = ((bf16[16,16,256]{2,1,0:T(8,128)(2,1)}), bf16[16,16,256]{2,1,0:T(8,128)(2,1)S(1)}, u32[]{:S(2)}, u32[]{:S(2)}) async-start(bf16[16,16,256]{2,1,0:T(8,128)(2,1)} %bitcast.20), calls=%async_computation.3 | async-start | bytes 262144 | tf_op jit(solution)/shard_map/all_to_all | solution.py:235
  119.8 12.2 %collective-permute-start.9 = (bf16[1,2,256,512]{3,2,1,0:T(8,128)(2,1)}, bf16[1,2,256,512]{3,2,1,0:T(8,128)(2,1)}, u32[]{:S(2)}, u32[]{:S(2)}) collective-permute-start(bf16[1,2,256,512]{3,2,1,0:T(8,128)(2,1)} %get-tuple-element.32), channel_id=1, source_target_pairs={{0,128},{128,0},{256,384},{384,256},{1,129},{129,1},{257,385},{385... | collective-permute-start | bytes 1572872 | tf_op jit(solution)/shard_map/ppermute | solution.py:227
  129.5 4.1 %collective-permute-start.11 = (bf16[1,2,256,512]{3,2,1,0:T(8,128)(2,1)}, bf16[1,2,256,512]{3,2,1,0:T(8,128)(2,1)}, u32[]{:S(2)}, u32[]{:S(2)}) collective-permute-start(bf16[1,2,256,512]{3,2,1,0:T(8,128)(2,1)} %collective-permute-done.10), channel_id=1, source_target_pairs={{0,128},{128,0},{256,384},{384,256},{1,129},{129,1},{257,385},{385... | collective-permute-start | bytes 1572872 | tf_op jit(solution)/shard_map/ppermute | solution.py:229
  137.4 13.5 %collective-permute-start.12 = (bf16[2,256,1024]{2,1,0:T(8,128)(2,1)}, bf16[2,256,1024]{2,1,0:T(8,128)(2,1)}, u32[]{:S(2)}, u32[]{:S(2)}) collective-permute-start(bf16[2,256,1024]{2,1,0:T(8,128)(2,1)} %collective-permute-done.8.refs_6_), channel_id=1, source_target_pairs={{0,128},{128,0},{256,384},{384,256},{1,129},{129,1},{257,385},{385... | collective-permute-start | bytes 3145736 | tf_op jit(solution)/shard_map/ppermute | solution.py:243
  143.7 17.4 %all-to-all-start.4 = ((bf16[8,128,256]{2,1,0:T(8,128)(2,1)}), bf16[8,128,256]{2,1,0:T(8,128)(2,1)}, u32[]{:S(2)}, u32[]{:S(2)}) async-start(bf16[8,128,256]{2,1,0:T(8,128)(2,1)} %broadcast_in_dim.36), calls=%async_computation.4 | async-start | bytes 1048576 | tf_op jit(solution)/shard_map/all_to_all | solution.py:244
  151.0 1.0 copy-start.4
  (1 other events, 0.8 us)
